TPU v7x, 128 devices: a whole 4x4x4 slice. The times are simulated.
128 devices in a mesh: psg: 32 (over x, y_lo, z), mp: 4 (over y_hi, core).
Axes of the slice: x: 4, y: 4 (y_hi: 2, y_lo: 2; y = y_hi * 2 + y_lo), z: 4, core: 2. Of those that a mesh axis runs over, the one named last changes fastest.
Arguments:
- tokens: bfloat16 [32768, 4096], P('psg'), may hold values from -6 to 6
- lengths: int32 [128], P('psg'), may hold values from 32 to 256, as said below
- assignment: int32 [128], P('psg'), may hold values from 0 to 3, as said below
- retrieval: float32 [128], P('psg'), may hold values from -8 to 306
- enc_gain: float32 [4096], replicated, may hold values from 0.25 to 1.75
- enc_qkv: bfloat16 [3, 4096, 2048], P(None, 'psg', 'mp'), may hold values from -0.09375 to 0.09375
- position_bias: float32 [32, 32], P('mp'), may hold values from -6 to 306
- enc_output: bfloat16 [2048, 4096], P('mp', 'psg'), may hold values from -0.125 to 0.125
- final_gain: float32 [4096], replicated, may hold values from 0.25 to 1.75
- embedding: bfloat16 [32128, 4096], P('mp', 'psg'), may hold values from -18 to 18
- dec_tokens: int32 [4, 2], replicated, may hold values from 0 to 32127
- dec_gain: float32 [4096], P('psg'), may hold values from 0.25 to 1.75
- cross_query: bfloat16 [4096, 2048], P('psg', 'mp'), may hold values from -0.0234375 to 0.0234375
- cross_keyval: bfloat16 [2, 4096, 2048], P(None, 'psg', 'mp'), may hold values from -0.09375 to 0.09375
- cross_output: bfloat16 [2048, 4096], P('mp', 'psg'), may hold values from -0.25 to 0.25
Outputs:
- encoded: bfloat16 [32768, 4096], P('psg', 'mp')
- decoded: bfloat16 [4, 2, 4096], P(None, None, ('psg', 'mp'))
Inputs may be any that keep to these rules, and one draw needn't show every extreme that they name: Passage p holds real tokens in its first lengths[p] slots and padding after them; in every draw all passages of some index of psg have 256 real tokens. `assignment`: every claim has exactly 32 passages.
All inputs are finite; a program needn't handle non-finite values.
Results may differ from a plain program's by a relative error of at most 0.013.
The roundings to bfloat16 on the way count: a program that leaves them out, or rounds other values in their place, can miss the bound.
Values may be sent and summed in bfloat16 or wider, within the bound.
A program may use at most 128 MiB of HBM per device.

v0:
```python
import math

import jax
import jax.numpy as jnp
import numpy as np
from jax import lax
from jax.sharding import PartitionSpec as P

D = 4096
HEAD_DIM = 64
BUCKETS = 32
MAXDIST = 128
SEQ = 256
CLAIMS = 4
POS = 2


EPSILON = 1e-06
MASKED = -1e30
HIGHEST = lax.Precision.HIGHEST


def merged(value, axis, combine):
    everything = jax.tree.map(lambda part: lax.all_gather(part, axis), value)
    first = jax.tree.map(lambda part: part[0], everything)

    def turn(k, so_far):
        return combine(so_far, jax.tree.map(lambda part: part[k], everything))

    return lax.fori_loop(1, lax.axis_size(axis), turn, first)


def bucket_onehot(length, buckets, max_distance):
    halfway = buckets // 2
    exact_max = halfway // 2
    relative_list = list(range(-(length - 1), length))
    beyond_list = [
        min(
            halfway - 1,
            exact_max
            + math.floor(
                math.log(max(abs(shift), 1) / exact_max)
                / math.log(max_distance / exact_max)
                * (halfway - exact_max)
            ),
        )
        for shift in relative_list
    ]
    relative = np.array(relative_list)
    beyond = np.array(beyond_list)
    distance = np.abs(relative)
    bucket_ids = np.where(relative > 0, halfway, 0) + np.where(
        distance < exact_max, distance, beyond
    )
    return (bucket_ids[None, :] == np.arange(buckets)[:, None]).astype(np.float32)


def toeplitz(vectors):
    heads_count, width_all = vectors.shape
    length = (width_all + 1) // 2
    padded = jnp.concatenate([vectors, jnp.zeros((heads_count, 1), vectors.dtype)], axis=1)
    rolled = jnp.roll(padded, -(length - 1), axis=1)
    repeated = jnp.tile(rolled, (1, length))[:, : length * (2 * length - 1)]
    return repeated.reshape(heads_count, length, 2 * length - 1)[:, :, :length]


def rms_norm(values, norm_gain):
    values = values.astype(jnp.float32)
    inverse = lax.rsqrt(jnp.mean(values * values, axis=-1, keepdims=True) + EPSILON)
    return values * inverse * norm_gain


def combine_partial(first, second):
    first_max, first_total, first_acc = first
    second_max, second_total, second_acc = second
    joint_max = jnp.maximum(first_max, second_max)
    first_scale = jnp.exp(first_max - joint_max)
    second_scale = jnp.exp(second_max - joint_max)
    joint_total = first_total * first_scale + second_total * second_scale
    joint_acc = first_acc * first_scale[..., None] + second_acc * second_scale[..., None]
    return (joint_max, joint_total, joint_acc)


def shards(
    tokens,
    lengths,
    assignment,
    retrieval,
    enc_gain,
    enc_qkv,
    position_bias,
    enc_output,
    final_gain,
    embedding,
    dec_tokens,
    dec_gain,
    cross_query,
    cross_keyval,
    cross_output,
):
    tok_rows = tokens.shape[0]
    model_width = tokens.shape[1]
    passages_here = lengths.shape[0]
    inner_here = enc_qkv.shape[2]
    heads_here = inner_here // HEAD_DIM
    query_rows = CLAIMS * POS
    positions = jnp.arange(SEQ)
    groups_count = lax.axis_size("mp")
    normed = rms_norm(tokens, enc_gain).astype(jnp.bfloat16)
    columns = normed
    projected = jnp.einsum(
        "td,kdc->ktc",
        columns,
        lax.all_gather(enc_qkv, "psg", axis=1, tiled=True),
        preferred_element_type=jnp.float32,
    )
    shaped = projected.astype(jnp.bfloat16).reshape(3, passages_here, SEQ, heads_here, HEAD_DIM)
    bias_table = jnp.dot(
        position_bias, jnp.asarray(bucket_onehot(SEQ, BUCKETS, MAXDIST)), precision=HIGHEST
    )
    pair_bias = toeplitz(bias_table)
    scores = (
        jnp.einsum("pihd,pjhd->phij", shaped[0], shaped[1], preferred_element_type=jnp.float32)
        + pair_bias[None]
    )
    valid_keys = positions[None, :] < lengths[:, None]
    scores = jnp.where(valid_keys[:, None, None, :], scores, MASKED)
    weights = jnp.exp(scores - jnp.max(scores, axis=-1, keepdims=True))
    probabilities = (weights / jnp.sum(weights, axis=-1, keepdims=True)).astype(jnp.bfloat16)
    attended = jnp.einsum(
        "phij,pjhd->pihd", probabilities, shaped[2], preferred_element_type=jnp.float32
    )
    attended = attended.astype(jnp.bfloat16).reshape(tok_rows, inner_here)
    share_width = model_width // groups_count
    share_start = lax.axis_index("mp") * share_width
    partial_out = jnp.dot(
        attended,
        lax.all_gather(enc_output, "psg", axis=1, tiled=True),
        preferred_element_type=jnp.float32,
    ).astype(jnp.bfloat16)
    summed = lax.psum(partial_out, "mp").astype(jnp.float32)
    encoded_full = (tokens.astype(jnp.float32) + summed).astype(jnp.bfloat16)
    encoded = lax.dynamic_slice_in_dim(encoded_full, share_start, share_width, 1)
    memory = rms_norm(encoded_full, final_gain).astype(jnp.bfloat16)
    vocab_here = embedding.shape[0]
    token_ids = dec_tokens.reshape(-1) - lax.axis_index("mp") * vocab_here
    lookup = (token_ids[:, None] == jnp.arange(vocab_here)[None, :]).astype(jnp.bfloat16)
    found_rows = jnp.dot(lookup, embedding, preferred_element_type=jnp.float32).astype(jnp.bfloat16)
    embedded = lax.psum(found_rows, "mp").astype(jnp.float32)
    query_weight = cross_query.astype(jnp.float32)
    squares_dec = lax.psum(jnp.sum(embedded * embedded, axis=1), "psg")
    dquery = embedded * lax.rsqrt(squares_dec / D + EPSILON)[:, None] * dec_gain
    cquery = lax.psum(jnp.dot(dquery, query_weight, precision=HIGHEST), "psg")
    cquery = cquery.reshape(query_rows, heads_here, HEAD_DIM)
    row_claim = jnp.arange(query_rows) // POS
    usable = (row_claim[:, None, None] == assignment[None, :, None]) & (
        positions[None, None, :] < lengths[None, :, None]
    )
    usable = usable.reshape(query_rows, 1, tok_rows)
    key_bias = jnp.broadcast_to(retrieval[:, None], (passages_here, SEQ)).reshape(tok_rows)
    columns = memory
    keyval = jnp.einsum(
        "td,kdc->ktc",
        columns,
        lax.all_gather(cross_keyval, "psg", axis=1, tiled=True),
        preferred_element_type=jnp.float32,
    )
    key_heads = keyval[0].reshape(tok_rows, heads_here, HEAD_DIM)
    value_heads = keyval[1].reshape(tok_rows, heads_here, HEAD_DIM)
    cross_scores = jnp.einsum("rhd,thd->rht", cquery, key_heads, precision=HIGHEST) + key_bias
    masked = jnp.where(usable, cross_scores, MASKED)
    local_max = jnp.max(masked, axis=-1)
    weights_c = jnp.where(usable, jnp.exp(masked - local_max[..., None]), 0.0)
    local_max, weights_c = (local_max, weights_c)
    local_total = jnp.sum(weights_c, axis=-1)
    local_acc = jnp.einsum("rht,thd->rhd", weights_c, value_heads, precision=HIGHEST)
    joint_max, joint_total, joint_acc = merged(
        (local_max, local_total, local_acc), "psg", combine_partial
    )
    cross_attn = joint_acc / joint_total[..., None]
    out_part = jnp.dot(
        cross_attn.reshape(query_rows, inner_here),
        cross_output.astype(jnp.float32),
        precision=HIGHEST,
    )
    out_share = lax.psum_scatter(out_part, "mp", scatter_dimension=1, tiled=True)
    piece_width = out_share.shape[1]
    residual = lax.dynamic_slice_in_dim(
        embedded, lax.axis_index("mp") * piece_width, piece_width, 1
    )
    decoded = (residual + out_share).astype(jnp.bfloat16).reshape(CLAIMS, POS, piece_width)
    return (encoded, decoded)


def solution(mesh):
    in_specs = (
        P("psg", None),
        P("psg"),
        P("psg"),
        P("psg"),
        P(),
        P(None, "psg", "mp"),
        P("mp", None),
        P("mp", "psg"),
        P(),
        P("mp", "psg"),
        P(),
        P("psg"),
        P("psg", "mp"),
        P(None, "psg", "mp"),
        P("mp", "psg"),
    )
    out_specs = (P("psg", "mp"), P(None, None, ("psg", "mp")))
    return jax.shard_map(shards, mesh=mesh, in_specs=in_specs, out_specs=out_specs, check_vma=False)
```

profile of v0, /device:TPU:1, one launch (start us, length us, event | category | flops | bytes accessed | tf_op | source)
XLA Modules:
  0.0 966.3 jit_solution(8447807892337837940)
XLA Ops:
  12.6 7.9 reshape.164
  20.5 3.1 slice.62
  26.7 5.1 fusion.8
  31.7 140.5 %all-gather.7.cloned.1.call-done = bf16[3,4096,512]{2,1,0:T(8,128)(2,1)} async-done(((bf16[3,128,512]{2,1,0:T(8,128)(2,1)}), bf16[3,4096,512]{2,1,0:T(8,128)(2,1)}) %all-gather.7.cloned.1.call-update) | async-done | bytes 12582928 | tf_op jit(solution)/shard_map/all_gather | solution.py:114
  172.3 18.3 %convert_bitcast_fusion = bf16[3,1024,512]{2,1,0:T(8,128)(2,1)S(1)} fusion(bf16[3,4096,512]{2,1,0:T(8,128)(2,1)} %all-gather.7.cloned.1.call-done, bf16[1024,4096]{1,0:T(8,128)(2,1)} %param.18, f32[4096]{0:T(1024)S(1)} %copy-done.9, f32[1024]{0:T(1024)S(1)} %add_rsqrt_fusion.1), kind=kOutput, calls=%fused_computation.40 | convolution fusion | flops 12903251968 | bytes 24137728 | tf_op jit(solution)/shard_map/td,kdc->ktc/dot_general | solution.py:111
  192.1 3.9 reshape.181
  196.0 3.9 reshape.182
  201.9 3.6 fusion.32
  205.6 5.3 fusion.61
  210.9 4.4 fusion.39
  216.4 92.2 %all-gather.9.cloned.1.call-done = bf16[512,4096]{1,0:T(8,128)(2,1)} async-done(((bf16[512,128]{1,0:T(8,128)(2,1)}), bf16[512,4096]{1,0:T(8,128)(2,1)}) %all-gather.9.cloned.1.call-update) | async-done | bytes 4194320 | tf_op jit(solution)/shard_map/all_gather | solution.py:138
  308.5 8.9 convolution_convert_fusion
  320.0 24.5 %psum.29 = bf16[8,128]{1,0:T(8,128)(2,1)S(1)} all-reduce(bf16[8,128]{1,0:T(8,128)(2,1)S(1)} %convolution_convert_fusion.1), channel_id=1, replica_groups=mesh['psg'=32,'mp'=4] {'mp'}, use_global_device_ids=true, to_apply=%region_4.5 | all-reduce | flops 1024 | bytes 4096 | tf_op jit(solution)/shard_map/psum | solution.py:149
  344.6 70.0 %psum.30 = f32[8]{0:T(128)S(1)} all-reduce(f32[8]{0:T(128)S(1)} %multiply_reduce_fusion), channel_id=1, replica_groups=mesh['psg'=32,'mp'=4] {'psg'}, use_global_device_ids=true, to_apply=%region_7.8 | all-reduce | flops 8 | bytes 64 | tf_op jit(solution)/shard_map/psum | solution.py:151
  415.2 127.7 %psum.31 = f32[8,8,64]{2,0,1:T(8,128)S(1)} all-reduce(f32[8,8,64]{2,0,1:T(8,128)S(1)} %copy.90), channel_id=1, replica_groups=mesh['psg'=32,'mp'=4] {'psg'}, use_global_device_ids=true, to_apply=%region_8.9 | all-reduce | flops 4096 | bytes 32768 | tf_op jit(solution)/shard_map/psum | solution.py:153
  543.1 10.6 %fusion.5 = (f32[1024]{0:T(1024)S(1)}, bf16[1024,4096]{1,0:T(8,128)(2,1)}) fusion(bf16[1024,4096]{1,0:T(8,128)(2,1)} %all-reduce.3.cloned.1.call-done, bf16[1024,4096]{1,0:T(8,128)(2,1)} %param.18), kind=kLoop, calls=%fused_computation.16 | loop fusion | flops 29359104 | bytes 25169920 | tf_op jit(solution)/shard_map/reduce_sum | solution.py:69
  553.7 97.6 %all-gather.11.cloned.1.call-done = bf16[2,4096,512]{1,2,0:T(8,128)(2,1)} async-done(((bf16[2,128,512]{1,2,0:T(8,128)(2,1)}), bf16[2,4096,512]{1,2,0:T(8,128)(2,1)}) %all-gather.11.cloned.1.call-update) | async-done | bytes 8388624 | tf_op jit(solution)/shard_map/all_gather | solution.py:165
  651.3 12.9 %fusion.29 = f32[2,1024,512]{1,2,0:T(8,128)S(1)} fusion(bf16[2,4096,512]{1,2,0:T(8,128)(2,1)} %all-gather.11.cloned.1.call-done, bf16[1024,4096]{1,0:T(8,128)(2,1)} %get-tuple-element.235, f32[4096]{0:T(1024)S(1)} %copy-done.10, f32[1024]{0:T(1024)S(1)} %add_rsqrt_fusion), kind=kOutput, calls=%fused_computation.41 | convolution fusion | flops 8606711808 | bytes 20992000 | tf_op jit(solution)/shard_map/td,kdc->ktc/dot_general | solution.py:162
  667.5 3.5 convolution_bitcast_fusion.1
  671.0 72.6 %all-gather.2 = f32[256,8,64]{2,0,1:T(8,128)S(1)} all-gather(f32[8,8,64]{2,0,1:T(8,128)S(1)} %convolution_bitcast_fusion.1), channel_id=4, replica_groups=mesh['psg'=32,'mp'=4] {'psg'}, dimensions={0}, use_global_device_ids=true | all-gather | bytes 540672 | tf_op jit(solution)/shard_map/all_gather | solution.py:24
  743.6 62.1 %all-gather.1 = f32[256,8]{1,0:T(8,128)S(1)} all-gather(f32[8,8]{1,0:T(8,128)S(1)} %copy.92), channel_id=3, replica_groups=mesh['psg'=32,'mp'=4] {'psg'}, dimensions={0}, use_global_device_ids=true | all-gather | bytes 8448 | tf_op jit(solution)/shard_map/all_gather | solution.py:24
  805.7 63.6 %all-gather = f32[256,8]{1,0:T(8,128)S(1)} all-gather(f32[8,8]{1,0:T(8,128)S(1)} %copy.91), channel_id=2, replica_groups=mesh['psg'=32,'mp'=4] {'psg'}, dimensions={0}, use_global_device_ids=true | all-gather | bytes 8448 | tf_op jit(solution)/shard_map/all_gather | solution.py:24
  869.3 4.8 while.19
  878.4 80.0 %reduce-scatter.4.cloned.1.call-done = f32[32,8]{1,0:T(8,128)} async-done(((f32[128,8]{1,0:T(8,128)}), f32[32,8]{1,0:T(8,128)}) %reduce-scatter.4.cloned.1.call-update) | async-done | bytes 1040
  (180 shorter events, 29.1 us)
Async XLA Ops:
  7.2 312.4 %copy-start = (bf16[8032,128]{1,0:T(8,128)(2,1)S(1)}, bf16[8032,128]{1,0:T(8,128)(2,1)}, u32[]{:S(2)}) copy-start(bf16[8032,128]{1,0:T(8,128)(2,1)} %param.27) | copy-start | bytes 6168580
  7.2 165.1 %all-gather.7.cloned.1.call-start = ((), (), s32[]{:S(2)}) async-start(), calls=%async_computation.1 | async-start | bytes 12976128 | tf_op jit(solution)/shard_map/all_gather | solution.py:114
  7.9 300.6 %all-gather.9.cloned.1.call-start = ((), (), s32[]{:S(2)}) async-start(), calls=%async_computation.2 | async-start | bytes 4325376 | tf_op jit(solution)/shard_map/all_gather | solution.py:138
  8.7 534.4 %all-reduce.3.cloned.1.call-start = ((), (), s32[]{:S(2)}) async-start(), calls=%async_computation.3 | async-start | bytes 16777216 | tf_op jit(solution)/shard_map/psum | solution.py:141
  12.6 13.9 %copy-start.7 = (s32[4]{0:T(128)S(1)}, s32[4]{0:T(128)}, u32[]{:S(2)}) copy-start(s32[4]{0:T(128)} %param.19) | copy-start | bytes 52
  20.5 151.7 %copy-start.9 = (f32[4096]{0:T(1024)S(1)}, f32[4096]{0:T(1024)}, u32[]{:S(2)}) copy-start(f32[4096]{0:T(1024)} %param.22) | copy-start | bytes 49156
  201.9 3.6 copy-start.2
  205.6 5.3 copy-start.1
  317.5 0.9 copy-start.3
  317.5 1.9 copy-start.5
  317.5 97.2 %copy-start.8 = (bf16[128,512]{1,0:T(8,128)(2,1)S(1)}, bf16[128,512]{1,0:T(8,128)(2,1)}, u32[]{:S(2)}) copy-start(bf16[128,512]{1,0:T(8,128)(2,1)} %param.30) | copy-start | bytes 393220
  317.5 97.2 %copy-start.11 = (f32[128]{0:T(128)S(1)}, f32[128]{0:T(128)}, u32[]{:S(2)}) copy-start(f32[128]{0:T(128)} %param.29) | copy-start | bytes 1540
  317.5 97.5 %copy-start.6 = (f32[4]{0:T(128)S(1)}, f32[4]{0:T(128)}, u32[]{:S(2)}) copy-start(f32[4]{0:T(128)} %param.21) | copy-start | bytes 52
  317.5 225.4 %copy-start.12 = (s32[4]{0:T(128)S(1)}, s32[4]{0:T(128)}, u32[]{:S(2)}) copy-start(s32[4]{0:T(128)} %param.20) | copy-start | bytes 52
  317.5 333.8 %all-gather.11.cloned.1.call-start = ((), (), s32[]{:S(2)}) async-start(), calls=%async_computation.4 | async-start | bytes 8650752 | tf_op jit(solution)/shard_map/all_gather | solution.py:165
  319.3 639.1 %reduce-scatter.4.cloned.1.call-start = ((), (), s32[]{:S(2)}) async-start(), calls=%async_computation.5 | async-start | bytes 81920
  543.1 108.2 %copy-start.10 = (f32[4096]{0:T(1024)S(1)}, f32[4096]{0:T(1024)}, u32[]{:S(2)}) copy-start(f32[4096]{0:T(1024)} %param.26) | copy-start | bytes 49156
  664.2 210.1 %copy-start.4 = (bf16[512,128]{1,0:T(8,128)(2,1)S(1)}, bf16[512,128]{1,0:T(8,128)(2,1)}, u32[]{:S(2)}) copy-start(bf16[512,128]{1,0:T(8,128)(2,1)} %param.32) | copy-start | bytes 393220
Sparse Core Ops, SparseCore 0:
  9.7 162.5 all-gather.6
  173.8 134.6 all-gather.8
  317.7 181.3 all-reduce.2
  501.0 150.2 all-gather.10
  875.4 82.9 reduce-scatter.3
where the time goes:
time: 967 us; the launch traced here: 966 us
  blocking collectives  420 us (43%)
  waiting for transfers between devices  412 us (43%)
  matrix products  55.5 us (6%)
  local copies, waits for them, and re-layouts  37.7 us (4%)
  other arithmetic  25.6 us (3%)
  between operations  14 us (1%)
    all_gather x3, blocking collectives, merged(): everything = jax.tree.map(lambda part: lax.all_gather(part, axis), value)  198 us
    all_gather x1, waiting for transfers between devices, shards(): lax.all_gather(enc_qkv, 'psg', axis=1, tiled=True)  141 us
    psum x1, blocking collectives, shards(): cquery = lax.psum(jnp.dot(dquery, query_weight, precision=HIGHEST), 'psg')  128 us
    all_gather x1, waiting for transfers between devices, shards(): lax.all_gather(cross_keyval, 'psg', axis=1, tiled=True)  97.6 us
    all_gather x1, waiting for transfers between devices, shards(): lax.all_gather(enc_output, 'psg', axis=1, tiled=True)  92.2 us
    unnamed x6, waiting for transfers between devices  81.4 us
    psum x1, blocking collectives, shards(): squares_dec = lax.psum(jnp.sum(embedded * embedded, axis=1), 'psg')  70 us
    psum x1, blocking collectives, shards(): embedded = lax.psum(found_rows, 'mp').astype(jnp.float32)  24.5 us
  transfers between devices with their start and end apart: 5, of which 4 were waited for; matrix products, arithmetic and copies ran while one was open for 9% of the time, Pallas kernels for 0%

commit v1 on v0

v1 whole, which is shorter than its diff:
```python
import functools
import math

import jax
import jax.numpy as jnp
import numpy as np
from jax import lax
from jax.experimental import pallas as pl
from jax.experimental.pallas import tpu as pltpu
from jax.sharding import PartitionSpec as P

D = 4096
HEAD_DIM = 64
BUCKETS = 32
MAXDIST = 128
SEQ = 256
CLAIMS = 4
POS = 2
NPSG = 32
NMP = 4
EPSILON = 1e-06
MASKED = -1e30
HIGHEST = lax.Precision.HIGHEST
MESH = pl.DeviceIdType.MESH
ANY = pl.BlockSpec(memory_space=pl.ANY)
VMEM = pl.BlockSpec(memory_space=pltpu.VMEM)


def bucket_onehot(length, buckets, max_distance):
    halfway = buckets // 2
    exact_max = halfway // 2
    relative_list = list(range(-(length - 1), length))
    beyond_list = [
        min(
            halfway - 1,
            exact_max
            + math.floor(
                math.log(max(abs(shift), 1) / exact_max)
                / math.log(max_distance / exact_max)
                * (halfway - exact_max)
            ),
        )
        for shift in relative_list
    ]
    relative = np.array(relative_list)
    beyond = np.array(beyond_list)
    distance = np.abs(relative)
    bucket_ids = np.where(relative > 0, halfway, 0) + np.where(
        distance < exact_max, distance, beyond
    )
    return (bucket_ids[None, :] == np.arange(buckets)[:, None]).astype(np.float32)


def toeplitz(vectors):
    heads_count, width_all = vectors.shape
    length = (width_all + 1) // 2
    padded = jnp.concatenate([vectors, jnp.zeros((heads_count, 1), vectors.dtype)], axis=1)
    rolled = jnp.roll(padded, -(length - 1), axis=1)
    repeated = jnp.tile(rolled, (1, length))[:, : length * (2 * length - 1)]
    return repeated.reshape(heads_count, length, 2 * length - 1)[:, :, :length]


def rms_norm(values, norm_gain):
    values = values.astype(jnp.float32)
    inverse = lax.rsqrt(jnp.mean(values * values, axis=-1, keepdims=True) + EPSILON)
    return values * inverse * norm_gain


def place():
    psg = lax.axis_index("psg")
    mp = lax.axis_index("mp")
    return psg // 8, (psg // 4) % 2, psg % 4, mp // 2, mp % 2


def psg_of(x, yl, z):
    return x * 8 + yl * 4 + z


def remote(src, dst, send_sem, recv_sem, device):
    return pltpu.make_async_remote_copy(
        src_ref=src,
        dst_ref=dst,
        send_sem=send_sem,
        recv_sem=recv_sem,
        device_id=device,
        device_id_type=MESH,
    )


def signal(device):
    pl.semaphore_signal(
        pltpu.get_barrier_semaphore(), inc=1, device_id=device, device_id_type=MESH
    )


def psg_gather_kernel(src, out, send_sem, recv_sem, own_sem):
    me = lax.axis_index("psg")
    mp = lax.axis_index("mp")

    def greet(k, c):
        signal((lax.rem(me + k, NPSG), mp))
        return c

    lax.fori_loop(1, NPSG, greet, 0)
    own = pltpu.make_async_copy(src, out.at[me], own_sem)
    own.start()
    pl.semaphore_wait(pltpu.get_barrier_semaphore(), NPSG - 1)

    def copy(k):
        return remote(
            src, out.at[me], send_sem.at[k], recv_sem.at[k], (lax.rem(me + k, NPSG), mp)
        )

    def start(k, c):
        copy(k).start()
        return c

    lax.fori_loop(1, NPSG, start, 0)

    def finish(k, c):
        copy(k).wait()
        return c

    lax.fori_loop(1, NPSG, finish, 0)
    own.wait()


def psg_gather(x, collective_id):
    return pl.pallas_call(
        psg_gather_kernel,
        out_shape=jax.ShapeDtypeStruct((NPSG,) + x.shape, x.dtype),
        in_specs=[VMEM],
        out_specs=VMEM,
        scratch_shapes=[
            pltpu.SemaphoreType.DMA((NPSG,)),
            pltpu.SemaphoreType.DMA((NPSG,)),
            pltpu.SemaphoreType.DMA,
        ],
        compiler_params=pltpu.CompilerParams(
            collective_id=collective_id, has_side_effects=True
        ),
    )(x)


def mp_exchange_kernel(split, src, out, send_sem, recv_sem, own_sem):
    psg = lax.axis_index("psg")
    me = lax.axis_index("mp")
    for k in range(1, NMP):
        signal((psg, lax.rem(me + k, NMP)))
    own = pltpu.make_async_copy(src.at[me] if split else src, out.at[me], own_sem)
    own.start()
    pl.semaphore_wait(pltpu.get_barrier_semaphore(), NMP - 1)
    copies = []
    for k in range(1, NMP):
        to = lax.rem(me + k, NMP)
        copies.append(
            remote(
                src.at[to] if split else src,
                out.at[me],
                send_sem.at[k],
                recv_sem.at[k],
                (psg, to),
            )
        )
        copies[-1].start()
    for copy in copies:
        copy.wait()
    own.wait()


def mp_exchange(x, collective_id, split):
    shape = x.shape if split else (NMP,) + x.shape
    return pl.pallas_call(
        functools.partial(mp_exchange_kernel, split),
        out_shape=jax.ShapeDtypeStruct(shape, x.dtype),
        in_specs=[VMEM],
        out_specs=VMEM,
        scratch_shapes=[
            pltpu.SemaphoreType.DMA((NMP,)),
            pltpu.SemaphoreType.DMA((NMP,)),
            pltpu.SemaphoreType.DMA,
        ],
        compiler_params=pltpu.CompilerParams(
            collective_id=collective_id, has_side_effects=True
        ),
    )(x)


def spread_kernel(src, out, send_sem, recv_sem, own_sem):
    psg = lax.axis_index("psg")
    mp = lax.axis_index("mp")
    x = psg // 8
    mine = x == mp

    def greet(k, c):
        frm = lax.rem(psg + k, NPSG)

        @pl.when(jnp.logical_or(k > 0, jnp.logical_not(mine)))
        def _():
            signal((frm, x))

        return c

    lax.fori_loop(0, NPSG, greet, 0)
    first = lax.rem(psg, 8) * 4 + mp

    def copy(k):
        t = lax.rem(first + k, NPSG)
        c, m = t // 4, lax.rem(t, 4)
        return remote(src.at[c, m], out.at[psg], send_sem.at[k], recv_sem.at[psg], (mp * 8 + c, m))

    @pl.when(mine)
    def _():
        own = pltpu.make_async_copy(src.at[lax.rem(psg, 8), mp], out.at[psg], own_sem)
        own.start()
        own.wait()
        pl.semaphore_wait(pltpu.get_barrier_semaphore(), NPSG - 1)

    @pl.when(jnp.logical_not(mine))
    def _():
        pl.semaphore_wait(pltpu.get_barrier_semaphore(), NPSG)
        copy(0).start()

    def start(k, c):
        copy(k).start()
        return c

    lax.fori_loop(1, NPSG, start, 0)

    def arrived(k, c):
        frm = lax.rem(psg + k, NPSG)
        remote(src.at[0, 0], out.at[frm], send_sem.at[0], recv_sem.at[frm], (frm, x)).wait_recv()
        return c

    def sent(k, c):
        copy(k).wait_send()
        return c

    @pl.when(jnp.logical_not(mine))
    def _():
        arrived(0, 0)
        copy(0).wait_send()

    lax.fori_loop(1, NPSG, arrived, 0)
    lax.fori_loop(1, NPSG, sent, 0)


def spread(x, collective_id):
    return pl.pallas_call(
        spread_kernel,
        out_shape=jax.ShapeDtypeStruct((NPSG,) + x.shape[2:], x.dtype),
        in_specs=[VMEM],
        out_specs=VMEM,
        scratch_shapes=[
            pltpu.SemaphoreType.DMA((NPSG,)),
            pltpu.SemaphoreType.DMA((NPSG,)),
            pltpu.SemaphoreType.DMA,
        ],
        compiler_params=pltpu.CompilerParams(
            collective_id=collective_id, has_side_effects=True
        ),
    )(x)


ROWS_A = (0, 16)
ROWS_B = (16, 16)
ROWS_D = (32, 48)
ROWS_E = (80, 48)
ALL = slice(None)


def weights_kernel(w_ref, b_ref, g_ref, e_ref, send_sem, recv_sem, own_sem):
    x, yl, z, yh, core = place()
    psg = lax.axis_index("psg")
    mp = lax.axis_index("mp")
    y_dev = (psg_of(x, 1 - yl, z), mp)

    def dev(axis, step):
        if axis == "x":
            return (psg_of(lax.rem(x + step, 4), yl, z), mp)
        return (psg_of(x, yl, lax.rem(z + step, 4)), mp)

    same_half = (x // 2) == yh
    yl_to = jnp.where(same_half, yl, 1 - yl)

    def block_to(k):
        return (psg_of(lax.rem(x + k, 4), yl_to, z), x)

    mine = x == mp

    for axis in ("x", "z"):
        signal(dev(axis, 1))
        signal(dev(axis, 3))
    signal(y_dev)
    for m in range(NMP):
        own_half = (m // 2) == yh
        frm = psg_of(mp, jnp.where(own_half, yl, 1 - yl), z)

        @pl.when(jnp.logical_not(jnp.logical_and(mine, m == mp)))
        def _():
            signal((frm, m))

    own = pltpu.make_async_copy(w_ref, g_ref.at[:, x, yl, z], own_sem.at[0])
    own.start()

    def g(xs, ys, zs, rows, cols=None):
        c = ALL if cols is None else pl.ds(cols * 256, 256)
        return g_ref.at[:, xs, ys, zs, pl.ds(rows[0], rows[1]), c]

    def send(t, src, dst, device):
        copy = remote(src, dst, send_sem.at[t], recv_sem.at[t], device)
        copy.start()
        return copy

    sent = []

    class Ring:
        def __init__(self, t, axis, piece, first=None):
            self.t, self.axis, self.piece = t, axis, piece
            at = x if axis == "x" else z
            self.at = at
            src = piece(at) if first is None else first
            self.up = send(t, src, piece(at), dev(axis, 1))
            self.down = send(t + 1, src, piece(at), dev(axis, 3))
            sent.extend([self.up, self.down])

        def forward(self):
            below = lax.rem(self.at + 3, 4)
            above = lax.rem(self.at + 1, 4)
            self.up.wait_recv()
            self.f_up = send(
                self.t + 2, self.piece(below, 0), self.piece(below, 0), dev(self.axis, 1)
            )
            self.down.wait_recv()
            self.f_down = send(
                self.t + 3, self.piece(above, 1), self.piece(above, 1), dev(self.axis, 3)
            )
            sent.extend([self.f_up, self.f_down])

        def end(self):
            self.f_up.wait_recv()
            self.f_down.wait_recv()

    def w(rows):
        return w_ref.at[:, pl.ds(rows[0], rows[1]), :]

    pl.semaphore_wait(pltpu.get_barrier_semaphore(), jnp.where(mine, 8, 9))

    yd = send(0, w(ROWS_D), g(x, yl, z, ROWS_D), y_dev)
    ye = send(1, w(ROWS_E), g(x, yl, z, ROWS_E), y_dev)
    sent.extend([yd, ye])
    a1 = Ring(4, "x", lambda v, c=None: g(v, yl, z, ROWS_A, c), w(ROWS_A))
    b1 = Ring(8, "z", lambda v, c=None: g(x, yl, v, ROWS_B, c), w(ROWS_B))
    own.wait()
    a1.forward()
    b1.forward()
    a1.end()
    b1.end()
    a2 = Ring(12, "z", lambda v, c=None: g(ALL, yl, v, ROWS_A, c))
    b2 = Ring(16, "x", lambda v, c=None: g(v, yl, ALL, ROWS_B, c))
    yd.wait_recv()
    ye.wait_recv()
    d2 = Ring(20, "x", lambda v, c=None: g(v, ALL, z, ROWS_D, c))
    e2 = Ring(24, "z", lambda v, c=None: g(x, ALL, v, ROWS_E, c))
    a2.forward()
    b2.forward()
    a2.end()
    b2.end()
    ya = send(2, g(ALL, yl, ALL, ROWS_A), g(ALL, yl, ALL, ROWS_A), y_dev)
    yb = send(3, g(ALL, yl, ALL, ROWS_B), g(ALL, yl, ALL, ROWS_B), y_dev)
    sent.extend([ya, yb])
    d2.forward()
    e2.forward()
    d2.end()
    e2.end()
    d3 = Ring(28, "z", lambda v, c=None: g(ALL, ALL, v, ROWS_D, c))
    e3 = Ring(32, "x", lambda v, c=None: g(v, ALL, ALL, ROWS_E, c))

    def e(ms, yls, zs):
        col = pl.multiple_of((yls * 4 + zs) * 128, 128)
        return e_ref.at[ms, :, pl.ds(col, 128)]

    for k in range(4):
        def remote_send():
            remote(
                b_ref, e(mp, yl, z), send_sem.at[36 + k], recv_sem.at[40 + mp], block_to(k)
            ).start()

        if k == 0:

            @pl.when(mine)
            def _():
                pltpu.make_async_copy(b_ref, e(mp, yl, z), own_sem.at[1]).start()

            pl.when(jnp.logical_not(mine))(remote_send)
        else:
            remote_send()
    for m in range(NMP):
        got = remote(b_ref, e(m, yl, z), send_sem.at[36], recv_sem.at[40 + m], y_dev)
        self_block = jnp.logical_and(mine, m == mp)
        pl.when(jnp.logical_not(self_block))(got.wait_recv)

    @pl.when(mine)
    def _():
        pltpu.make_async_copy(b_ref, e(mp, yl, z), own_sem.at[1]).wait()

    near = pl.ds(yh * 2, 2)
    far = pl.ds(2 - yh * 2, 2)
    y1 = send(44, e(near, yl, z), e(near, yl, z), y_dev)
    y2 = send(45, e(far, 1 - yl, z), e(far, 1 - yl, z), y_dev)
    sent.extend([y1, y2])
    y1.wait_recv()
    y2.wait_recv()

    d3.forward()
    e3.forward()

    def e_piece(v, c=None):
        return e(ALL, c, v)

    rings = []
    for i in range(2):
        up = send(46 + i, e(ALL, i, z), e(ALL, i, z), dev("z", 1))
        down = send(48 + i, e(ALL, i, z), e(ALL, i, z), dev("z", 3))
        rings.append((up, down))
        sent.extend([up, down])
    below = lax.rem(z + 3, 4)
    above = lax.rem(z + 1, 4)
    rings[0][0].wait_recv()
    f_up = send(50, e(ALL, 0, below), e(ALL, 0, below), dev("z", 1))
    rings[1][1].wait_recv()
    f_down = send(51, e(ALL, 1, above), e(ALL, 1, above), dev("z", 3))
    sent.extend([f_up, f_down])
    rings[1][0].wait_recv()
    rings[0][1].wait_recv()
    ya.wait_recv()
    yb.wait_recv()
    d3.end()
    e3.end()
    f_up.wait_recv()
    f_down.wait_recv()
    for copy in sent:
        copy.wait_send()
    for k in range(4):
        done = remote(b_ref, e(mp, yl, z), send_sem.at[36 + k], recv_sem.at[40], y_dev)
        if k == 0:
            pl.when(jnp.logical_not(mine))(done.wait_send)
        else:
            done.wait_send()


def gather_weights(enc_qkv, block):
    return pl.pallas_call(
        weights_kernel,
        out_shape=(
            jax.ShapeDtypeStruct((3, 4, 2, 4, 128, 512), jnp.bfloat16),
            jax.ShapeDtypeStruct((NMP, block.shape[0], 1024), jnp.bfloat16),
        ),
        in_specs=[ANY, ANY],
        out_specs=(ANY, ANY),
        scratch_shapes=[
            pltpu.SemaphoreType.DMA((52,)),
            pltpu.SemaphoreType.DMA((52,)),
            pltpu.SemaphoreType.DMA((2,)),
        ],
        compiler_params=pltpu.CompilerParams(collective_id=1, has_side_effects=True),
    )(enc_qkv, block)


def attended_kernel(src, out, transit, send_sem, recv_sem, own_sem):
    x, yl, z, yh, core = place()
    psg = lax.axis_index("psg")
    mp = lax.axis_index("mp")
    half = src.shape[0] // 2
    y = yh * 2 + yl

    def dev(step, other_core=False):
        t = lax.rem(y + step, 4)
        c = 1 - core if other_core else core
        return (psg_of(x, lax.rem(t, 2), z), (t // 2) * 2 + c)

    for step in (1, 3):
        signal(dev(step))
    signal(dev(0, True))
    own = pltpu.make_async_copy(src, out.at[mp], own_sem)
    own.start()
    pl.semaphore_wait(pltpu.get_barrier_semaphore(), 3)
    far = (1 - yh) * 2 + core
    quarter = half // 2
    sent = []

    def send(t, s, d, device):
        copy = remote(s, d, send_sem.at[t], recv_sem.at[t], device)
        copy.start()
        sent.append(copy)
        return copy

    hops = []
    for q in range(2):
        for up in range(2):
            rows = pl.ds(up * half + q * quarter, quarter)
            hops.append(
                send(
                    q * 2 + up, src.at[rows], transit.at[up, pl.ds(q * quarter, quarter)],
                    dev(1 if up == 0 else 3),
                )
            )
    chip = send(8, src, out.at[mp], dev(0, True))
    ends = []
    y_src = [lax.rem(y + 3, 4), lax.rem(y + 1, 4)]
    for q in range(2):
        for up in range(2):
            hops[q * 2 + up].wait_recv()
            rows = pl.ds(up * half + q * quarter, quarter)
            slot = (y_src[up] // 2) * 2 + core
            ends.append(
                send(
                    4 + q * 2 + up, transit.at[up, pl.ds(q * quarter, quarter)],
                    out.at[slot, rows], dev(1 if up == 0 else 3),
                )
            )
    last = []
    for q in range(2):
        for up in range(2):
            ends[q * 2 + up].wait_recv()
            rows = pl.ds(up * half + q * quarter, quarter)
            last.append(
                send(9 + q * 2 + up, out.at[far, rows], out.at[far, rows], dev(0, True))
            )
    chip.wait_recv()
    for copy in last:
        copy.wait_recv()
    for copy in sent:
        copy.wait_send()
    own.wait()


def gather_attended(x):
    rows, cols = x.shape
    return pl.pallas_call(
        attended_kernel,
        out_shape=jax.ShapeDtypeStruct((NMP, rows, cols), x.dtype),
        in_specs=[VMEM],
        out_specs=VMEM,
        scratch_shapes=[
            pltpu.VMEM((2, rows // 2, cols), x.dtype),
            pltpu.SemaphoreType.DMA((13,)),
            pltpu.SemaphoreType.DMA((13,)),
            pltpu.SemaphoreType.DMA,
        ],
        compiler_params=pltpu.CompilerParams(
            collective_id=2, has_side_effects=True, vmem_limit_bytes=32 << 20
        ),
    )(x)


def high_low(values):
    high = values.astype(jnp.bfloat16)
    low = (values - high.astype(jnp.float32)).astype(jnp.bfloat16)
    return high, low


def shards(
    tokens,
    lengths,
    assignment,
    retrieval,
    enc_gain,
    enc_qkv,
    position_bias,
    enc_output,
    final_gain,
    embedding,
    dec_tokens,
    dec_gain,
    cross_query,
    cross_keyval,
    cross_output,
):
    f32 = jnp.float32
    psg = lax.axis_index("psg")
    mp = lax.axis_index("mp")
    tok_rows = tokens.shape[0]
    passages_here = lengths.shape[0]
    heads_here = enc_qkv.shape[2] // HEAD_DIM
    query_rows = CLAIMS * POS
    positions = jnp.arange(SEQ)

    vocab_here = embedding.shape[0]
    token_ids = dec_tokens.reshape(-1) - mp * vocab_here
    held = (token_ids >= 0) & (token_ids < vocab_here)
    row_ids = jnp.clip(token_ids, 0, vocab_here - 1)
    rows = [lax.dynamic_slice_in_dim(embedding, row_ids[i], 1, 0) for i in range(query_rows)]
    found = jnp.where(held[:, None], jnp.concatenate(rows, axis=0).astype(f32), 0.0)
    embedded = jnp.sum(mp_exchange(found, 3, False), axis=0)
    part = jnp.dot(embedded * dec_gain, cross_query.astype(f32), precision=HIGHEST)
    squares = jnp.sum(embedded * embedded, axis=1, keepdims=True)
    part = jnp.concatenate([part, jnp.broadcast_to(squares, (query_rows, 128))], axis=1)
    joined = jnp.sum(psg_gather(part, 4), axis=0)
    cquery = joined[:, :512] * lax.rsqrt(joined[:, 512:513] / D + EPSILON)
    folded = jnp.einsum(
        "rhd,chd->rhc",
        cquery.reshape(query_rows, heads_here, HEAD_DIM),
        cross_keyval[0].astype(f32).reshape(128, heads_here, HEAD_DIM),
        precision=HIGHEST,
    ).reshape(query_rows * heads_here, 128)
    gain_here = lax.dynamic_slice_in_dim(final_gain, psg * 128, 128, 0)
    high, low = high_low(folded * gain_here)
    block = jnp.concatenate([enc_output, high, low], axis=0)

    qkv_all, blocks = gather_weights(enc_qkv, block)
    qkv_all = qkv_all.reshape(3, D, 512)

    normed = rms_norm(tokens, enc_gain).astype(jnp.bfloat16)
    projected = jnp.einsum("td,kdc->ktc", normed, qkv_all, preferred_element_type=f32)
    shaped = projected.astype(jnp.bfloat16).reshape(3, passages_here, SEQ, heads_here, HEAD_DIM)
    bias_table = jnp.dot(
        position_bias, jnp.asarray(bucket_onehot(SEQ, BUCKETS, MAXDIST)), precision=HIGHEST
    )
    pair_bias = toeplitz(bias_table)
    scores = (
        jnp.einsum("pihd,pjhd->phij", shaped[0], shaped[1], preferred_element_type=f32)
        + pair_bias[None]
    )
    valid_keys = positions[None, :] < lengths[:, None]
    scores = jnp.where(valid_keys[:, None, None, :], scores, MASKED)
    weights = jnp.exp(scores - jnp.max(scores, axis=-1, keepdims=True))
    probabilities = (weights / jnp.sum(weights, axis=-1, keepdims=True)).astype(jnp.bfloat16)
    attended = jnp.einsum("phij,pjhd->pihd", probabilities, shaped[2], preferred_element_type=f32)
    attended = attended.astype(jnp.bfloat16).reshape(tok_rows, 512)

    groups = gather_attended(attended)
    width = blocks.shape[2]
    summed = jnp.zeros((tok_rows, width), f32)
    for m in range(NMP):
        summed = summed + jnp.dot(
            groups[m], blocks[m, :512], preferred_element_type=f32
        ).astype(jnp.bfloat16).astype(f32)
    tokens_here = lax.dynamic_slice_in_dim(tokens, mp * width, width, 1)
    encoded = (tokens_here.astype(f32) + summed).astype(jnp.bfloat16)
    encoded_f = encoded.astype(f32)
    squares = jnp.sum(encoded_f * encoded_f, axis=1).reshape(passages_here, SEQ)

    rows_u = blocks[:, 512:].reshape(NMP, 2, CLAIMS, POS * heads_here, width)
    claim_u = jnp.stack(
        [lax.dynamic_index_in_dim(rows_u, assignment[i], 2, False) for i in range(passages_here)],
        axis=2,
    )
    per_psg = encoded.reshape(passages_here, SEQ, width)
    partial = jnp.einsum("mapnd,pkd->mapnk", claim_u, per_psg, preferred_element_type=f32)
    partial = (partial[:, 0] + partial[:, 1]).reshape(NMP, passages_here * POS * heads_here, SEQ)
    extra = jnp.broadcast_to(
        jnp.concatenate([squares, jnp.zeros_like(squares)], axis=0)[None],
        (NMP, 2 * passages_here, SEQ),
    )
    raw = jnp.sum(mp_exchange(jnp.concatenate([partial, extra], axis=1), 5, True), axis=0)
    n_rows = passages_here * POS * heads_here
    inverse = lax.rsqrt(raw[n_rows : n_rows + passages_here] / D + EPSILON)
    cross = raw[:n_rows].reshape(passages_here, POS * heads_here, SEQ)
    cross = cross * inverse[:, None, :] + retrieval[:, None, None]
    usable = (positions[None, :] < lengths[:, None])[:, None, :]
    masked = jnp.where(usable, cross, MASKED)
    onehot = assignment[None, :] == jnp.arange(CLAIMS)[:, None]
    psg_max = jnp.max(masked, axis=-1)
    local_max = jnp.max(jnp.where(onehot[:, :, None], psg_max[None], MASKED), axis=1)
    chosen_max = jnp.max(jnp.where(onehot[:, :, None], local_max[:, None], MASKED), axis=0)
    weights_c = jnp.where(
        usable, jnp.exp(masked - chosen_max[:, :, None]), 0.0
    )
    local_total = jnp.sum(
        jnp.where(onehot[:, :, None], jnp.sum(weights_c, axis=-1)[None], 0.0), axis=1
    )
    stats = jnp.stack([local_max.reshape(-1), local_total.reshape(-1)])
    stats = jnp.pad(stats, ((0, 6), (0, SEQ - stats.shape[1])))
    sent = jnp.concatenate(
        [(weights_c * inverse[:, None, :]).reshape(n_rows, SEQ), stats], axis=0
    )
    all_w = mp_exchange(sent, 6, False)
    spread_w = jnp.where(
        onehot[None, :, :, None, None],
        all_w[:, :n_rows].reshape(NMP, 1, passages_here, POS * heads_here, SEQ),
        0.0,
    )
    w_high, w_low = high_low(spread_w)
    weighted = jnp.einsum(
        "mcpnk,pkd->mcnd", w_high, per_psg, preferred_element_type=f32
    ) + jnp.einsum("mcpnk,pkd->mcnd", w_low, per_psg, preferred_element_type=f32)
    weighted = weighted.reshape(NMP, query_rows * heads_here, 8, 128).transpose(2, 0, 1, 3)
    both = jnp.concatenate([all_w[:, n_rows, :64], all_w[:, n_rows + 1, :64]], axis=1)
    both = jnp.broadcast_to(
        jnp.pad(both[:, None, :], ((0, 0), (0, 7), (0, 0)))[None], (8, NMP, 8, 128)
    )
    got = spread(jnp.concatenate([weighted, both], axis=2), 7)
    each_max = got[:, 64, :64]
    each_total = got[:, 64, 64:]
    joint_max = jnp.max(each_max, axis=0)
    scale = jnp.exp(each_max - joint_max[None])
    total = jnp.sum(scale * each_total, axis=0)
    mean_rows = jnp.sum(got[:, :64] * scale[:, :, None], axis=0) / total[:, None] * gain_here
    attn_part = jnp.einsum(
        "rhc,chd->rhd",
        mean_rows.reshape(query_rows, heads_here, 128),
        cross_keyval[1].astype(f32).reshape(128, heads_here, HEAD_DIM),
        precision=HIGHEST,
    ).reshape(query_rows, 512)
    cross_attn = jnp.sum(psg_gather(attn_part, 8), axis=0)
    out_part = jnp.dot(cross_attn, cross_output.astype(f32), precision=HIGHEST)
    out_sum = jnp.sum(mp_exchange(out_part, 9, False), axis=0) + embedded
    decoded = lax.dynamic_slice_in_dim(out_sum, mp * 32, 32, 1)
    return (encoded, decoded.astype(jnp.bfloat16).reshape(CLAIMS, POS, 32))


def solution(mesh):
    in_specs = (
        P("psg", None),
        P("psg"),
        P("psg"),
        P("psg"),
        P(),
        P(None, "psg", "mp"),
        P("mp", None),
        P("mp", "psg"),
        P(),
        P("mp", "psg"),
        P(),
        P("psg"),
        P("psg", "mp"),
        P(None, "psg", "mp"),
        P("mp", "psg"),
    )
    out_specs = (P("psg", "mp"), P(None, None, ("psg", "mp")))
    return jax.shard_map(shards, mesh=mesh, in_specs=in_specs, out_specs=out_specs, check_vma=False)
```

time: 967 us -> 412 us (0.43)
  blocking collectives: 420 us -> 0 us
  waiting for transfers between devices: 412 us -> 0 us
  Pallas kernels: 0 us -> 273 us
  between operations: 14 us -> 23.8 us
    all_gather x3 -> x0, waiting for transfers between devices: 330 us -> none  [the longest x1 141 us: shards(): lax.all_gather(enc_qkv, 'psg', axis=1, tiled=True)]
    pallas_call x0 -> x9, Pallas kernels: none -> 273 us  [the longest x1 136 us: gather_weights(): pl.pallas_call(weights_kernel, out_shape=(jax.ShapeDtypeStruct((3, 4, 2,...]
    psum x3 -> x0, blocking collectives: 222 us -> none  [the longest x1 128 us: shards(): cquery = lax.psum(jnp.dot(dquery, query_weight, precision=HIGHEST), 'psg')]
    all_gather x3 -> x0, blocking collectives: 198 us -> none  [merged(): everything = jax.tree.map(lambda part: lax.all_gather(part, axis), value)]
    unnamed x6 -> x0, waiting for transfers between devices: 81.4 us -> none
    reduce_sum x2 -> x1, other arithmetic: 15.7 us -> 5.22 us  [rms_norm(): jnp.mean(values * values, axis=-1, keepdims=True) + EPSILON]
    dot_general x7 -> x12, matrix products: 45.5 us -> 38.9 us  [the longest x4 17.6 us: shards(): jnp.dot(groups[m], blocks[m, :512], preferred_element_type=f32)]
  transfers between devices with their start and end apart: 5 -> 0, of which waited for: 4 -> 0; matrix products, arithmetic and copies ran while one was open for 9% -> 0% of each run, Pallas kernels for 0% -> 0%
where the time goes in v1:
time: 412 us; the launch traced here: 410 us
  Pallas kernels  273 us (66%)
  matrix products  47.7 us (12%)
  local copies, waits for them, and re-layouts  33.6 us (8%)
  other arithmetic  31.9 us (8%)
  between operations  23.8 us (6%)
    pallas_call x1, Pallas kernels, gather_weights(): pl.pallas_call(weights_kernel, out_shape=(jax.ShapeDtypeStruct((3, 4, 2,...  136 us
    pallas_call x1, Pallas kernels, gather_attended(): pl.pallas_call(attended_kernel, out_shape=jax.ShapeDtypeStruct((NMP, rows...  39.6 us
    pallas_call x1, Pallas kernels, spread(): pl.pallas_call(spread_kernel, out_shape=jax.ShapeDtypeStruct((NPSG,) + x....  34 us
    pallas_call x4, Pallas kernels, mp_exchange(): pl.pallas_call(functools.partial(mp_exchange_kernel, split), out_shape=ja...  32.9 us
    pallas_call x2, Pallas kernels, psg_gather(): pl.pallas_call(psg_gather_kernel, out_shape=jax.ShapeDtypeStruct((NPSG,)...  30.5 us
    dot_general x4, matrix products, shards(): jnp.dot(groups[m], blocks[m, :512], preferred_element_type=f32)  17.6 us
    dot_general x1, matrix products, shards(): jnp.einsum('td,kdc->ktc', normed, qkv_all, preferred_element_type=f32)  16.9 us
    sub x1, other arithmetic, shards(): weights = jnp.exp(scores - jnp.max(scores, axis=-1, keepdims=True))  12.3 us

profile of v1, /device:TPU:1, one launch (start us, length us, event | category | flops | bytes accessed | tf_op | source)
XLA Modules:
  0.0 410.4 jit_solution(8455670437659606802)
XLA Ops:
  21.0 7.4 %shard_map.167 = f32[4,8,128]{2,1,0:T(8,128)} custom-call(f32[8,128]{1,0:T(8,128)} %convert_select_fusion.src), custom_call_target="tpu_custom_call" | custom-call | tf_op jit(solution)/shard_map/pallas_call | solution.py:173
  30.7 16.9 %shard_map.168 = f32[32,8,640]{2,1,0:T(8,128)} custom-call(f32[8,640]{1,0:T(8,128)} %pad_maximum_fusion.4.src), custom_call_target="tpu_custom_call" | custom-call | tf_op jit(solution)/shard_map/pallas_call | solution.py:129
  50.1 1.6 pad_maximum_fusion.2.b_ref
  51.7 136.2 %shard_map.169 = (bf16[3,4,2,4,128,512]{5,4,3,2,1,0:T(8,128)(2,1)}, bf16[4,640,1024]{2,1,0:T(8,128)(2,1)}) custom-call(bf16[3,128,512]{2,1,0:T(8,128)(2,1)} %w_ref.1, bf16[640,128]{1,0:T(8,128)(2,1)} %pad_maximum_fusion.2.b_ref), custom_call_target="tpu_custom_call" | custom-call | tf_op jit(solution)/shard_map/pallas_call | solution.py:453
  188.0 5.2 %fusion.1 = f32[1024]{0:T(1024)S(1)} fusion(bf16[1024,4096]{1,0:T(8,128)(2,1)} %param.16), kind=kLoop, calls=%fused_computation.3 | loop fusion | flops 12581888 | bytes 8392704 | tf_op jit(solution)/shard_map/reduce_sum | solution.py:65
  193.7 16.9 %convert_bitcast_fusion = bf16[3,1024,512]{1,2,0:T(8,128)(2,1)S(1)} fusion(bf16[3,4096,512]{2,1,0:T(8,128)(2,1)} %bitcast.181, bf16[1024,4096]{1,0:T(8,128)(2,1)S(1)} %copy-done.3, f32[4096]{0:T(1024)S(1)} %copy-done.9, f32[1024]{0:T(1024)S(1)} %add_rsqrt_fusion), kind=kOutput, calls=%fused_computation.20 | convolution fusion | flops 12903251968 | bytes 24137728 | tf_op jit(solution)/shard_map/td,kdc->ktc/dot_general | solution.py:615
  212.7 1.9 squeeze.99
  214.6 4.5 %fusion.39 = f32[4,8,256,256]{2,3,1,0:T(8,128)} fusion(bf16[4,256,8,64]{1,0,3,2:T(4,128)(2,1)S(1)} %squeeze.100, bf16[4,256,8,64]{1,0,3,2:T(4,128)(2,1)S(1)} %squeeze.99), kind=kOutput, calls=%fused_computation.54 | convolution fusion | flops 268435456 | bytes 10485760 | tf_op jit(solution)/shard_map/pihd,pjhd->phij/dot_general | solution.py:622
  220.0 2.2 slice.180
  222.2 7.9 %reshape.227 = f32[8,256,511]{2,1,0:T(8,128)} reshape(f32[8,130816]{1,0:T(8,128)} %slice.180) | data formatting | bytes 8372224 | tf_op jit(solution)/shard_map/reshape | solution.py:60
  230.1 1.6 slice-done
  231.7 1.8 copy.123
  233.6 12.3 %fusion.82 = (f32[4,8,256]{2,1,0:T(8,128)S(1)}, f32[4,8,256,256]{2,3,1,0:T(8,128)}) fusion(f32[4,8,256,256]{2,3,1,0:T(8,128)} %fusion.39, f32[8,256,256]{1,2,0:T(8,128)} %copy.123, pred[4,256]{1,0:T(4,128)(4,1)S(1)} %iota_compare_fusion.2), kind=kOutput, calls=%fused_computation.143 | output fusion | flops 12583167 | bytes 18908160 | tf_op jit(solution)/shard_map/sub | solution.py:627
  246.7 4.2 %fusion.17 = bf16[4,256,8,64]{1,3,2,0:T(8,128)(2,1)S(1)} fusion(f32[4,8,256,256]{2,3,1,0:T(8,128)} %get-tuple-element.46, f32[4,8,256]{2,1,0:T(8,128)S(1)} %get-tuple-element.45, bf16[4,256,8,64]{1,0,3,2:T(4,128)(2,1)S(1)} %squeeze.98), kind=kOutput, calls=%fused_computation.26 | convolution fusion | flops 273154048 | bytes 10518528 | tf_op jit(solution)/shard_map/phij,pjhd->pihd/dot_general | solution.py:629
  253.3 39.6 %shard_map.170 = bf16[4,1024,512]{2,1,0:T(8,128)(2,1)S(1)} custom-call(bf16[1024,512]{1,0:T(8,128)(2,1)S(1)} %reshape.240.src), custom_call_target="tpu_custom_call" | custom-call | tf_op jit(solution)/shard_map/pallas_call | solution.py:540
  293.0 3.3 fusion.29
  296.3 3.8 fusion.32
  300.1 3.8 fusion.35
  303.9 6.7 %multiply_reduce_fusion = (f32[1024]{0:T(1024)S(1)}, bf16[1024,1024]{1,0:T(8,128)(2,1)}) fusion(bf16[4,640,1024]{2,1,0:T(8,128)(2,1)} %get-tuple-element.5, bf16[4,1024,512]{2,1,0:T(8,128)(2,1)} %copy-done.2, bf16[1024,1024]{1,0:T(8,128)(2,1)S(1)} %fusion.29, bf16[1024,1024]{1,0:T(8,128)(2,1)} %fusion.32, bf16[1024,1024]{1,0:T(8,128)(2,1)} %fusion.35, ...), kind=kOutput, calls=%fused_computation.14 | convolution fusion | flops 1088420864 | bytes 12587012 | tf_op jit(solution)/shard_map/dot_general | solution.py:636
  322.3 8.9 %shard_map.171 = f32[4,72,256]{2,1,0:T(8,128)} custom-call(f32[4,72,256]{2,1,0:T(8,128)} %pad_maximum_fusion.1.src), custom_call_target="tpu_custom_call" | custom-call | tf_op jit(solution)/shard_map/pallas_call | solution.py:173
  334.1 8.8 %shard_map.172 = f32[4,72,256]{2,1,0:T(8,128)} custom-call(f32[72,256]{1,0:T(8,128)} %pad_maximum_fusion.3.src), custom_call_target="tpu_custom_call" | custom-call | tf_op jit(solution)/shard_map/pallas_call | solution.py:173
  347.9 34.0 %shard_map.173 = f32[32,72,128]{2,1,0:T(8,128)} custom-call(f32[8,4,72,128]{3,2,1,0:T(8,128)} %pad_maximum_fusion.src), custom_call_target="tpu_custom_call" | custom-call | tf_op jit(solution)/shard_map/pallas_call | solution.py:249
  385.8 13.5 %shard_map.174 = f32[32,8,512]{2,1,0:T(8,128)} custom-call(f32[8,512]{1,0:T(8,128)} %reshape.234.src), custom_call_target="tpu_custom_call" | custom-call | tf_op jit(solution)/shard_map/pallas_call | solution.py:129
  401.2 7.8 %shard_map.175 = f32[4,8,128]{2,1,0:T(8,128)} custom-call(f32[8,128]{1,0:T(8,128)} %fusion.83.src), custom_call_target="tpu_custom_call" | custom-call | tf_op jit(solution)/shard_map/pallas_call | solution.py:173
  (113 shorter events, 35.6 us)
Async XLA Ops:
  0.6 28.7 %copy-start = (bf16[128,512]{1,0:T(8,128)(2,1)S(1)}, bf16[128,512]{1,0:T(8,128)(2,1)}, u32[]{:S(2)}) copy-start(bf16[128,512]{1,0:T(8,128)(2,1)} %param.28) | copy-start | bytes 393220
  51.7 141.5 %copy-start.9 = (f32[4096]{0:T(1024)S(1)}, f32[4096]{0:T(1024)}, u32[]{:S(2)}) copy-start(f32[4096]{0:T(1024)} %param.20) | copy-start | bytes 49156
  187.9 5.8 %copy-start.3 = (bf16[1024,4096]{1,0:T(8,128)(2,1)S(1)}, bf16[1024,4096]{1,0:T(8,128)(2,1)}, u32[]{:S(2)}) copy-start(bf16[1024,4096]{1,0:T(8,128)(2,1)} %param.16) | copy-start | bytes 25165828
  214.6 4.6 %copy-start.5 = (f32[32,511]{1,0:T(8,128)S(1)}, f32[32,511]{1,0:T(8,128)}, u32[]{:S(2)}) copy-start(f32[32,511]{1,0:T(8,128)} %constant.58.clone) | copy-start | bytes 196228
  214.6 4.5 %copy-start.7 = (f32[8,32]{1,0:T(8,128)S(1)}, f32[8,32]{1,0:T(8,128)}, u32[]{:S(2)}) copy-start(f32[8,32]{1,0:T(8,128)} %param.22) | copy-start | bytes 3076
  230.1 1.6 slice-start
  230.1 3.4 copy-start.10
  293.0 7.1 %copy-start.2 = (bf16[4,1024,512]{2,1,0:T(8,128)(2,1)}, bf16[4,1024,512]{2,1,0:T(8,128)(2,1)S(1)}, u32[]{:S(2)}) copy-start(bf16[4,1024,512]{2,1,0:T(8,128)(2,1)S(1)} %shard_map.170) | copy-start | bytes 12582916
  303.9 8.4 %copy-start.6 = (s32[4]{0:T(128)S(1)}, s32[4]{0:T(128)}, u32[]{:S(2)}) copy-start(s32[4]{0:T(128)} %param.18) | copy-start | bytes 52
  310.7 9.8 %copy-start.11 = (bf16[1024,1024]{1,0:T(8,128)(2,1)S(1)}, bf16[1024,1024]{1,0:T(8,128)(2,1)}, u32[]{:S(2)}) copy-start(bf16[1024,1024]{1,0:T(8,128)(2,1)} %get-tuple-element.48) | copy-start | bytes 6291460
  320.6 11.6 %copy-start.8 = (f32[4]{0:T(128)S(1)}, f32[4]{0:T(128)}, u32[]{:S(2)}) copy-start(f32[4]{0:T(128)} %param.19) | copy-start | bytes 52
  346.5 63.9 %copy-start.1 = (bf16[128,512]{1,0:T(8,128)(2,1)S(1)}, bf16[128,512]{1,0:T(8,128)(2,1)}, u32[]{:S(2)}) copy-start(bf16[128,512]{1,0:T(8,128)(2,1)} %param.28) | copy-start | bytes 393220
  346.7 53.7 %copy-start.4 = (bf16[512,128]{1,0:T(8,128)(2,1)S(1)}, bf16[512,128]{1,0:T(8,128)(2,1)}, u32[]{:S(2)}) copy-start(bf16[512,128]{1,0:T(8,128)(2,1)} %param.30) | copy-start | bytes 393220

commit v2 on v1

v2 whole, which is shorter than its diff:
```python
import functools
import math

import jax
import jax.numpy as jnp
import numpy as np
from jax import lax
from jax.experimental import pallas as pl
from jax.experimental.pallas import tpu as pltpu
from jax.sharding import PartitionSpec as P

D = 4096
HEAD_DIM = 64
BUCKETS = 32
MAXDIST = 128
SEQ = 256
CLAIMS = 4
POS = 2
NPSG = 32
NMP = 4
EPSILON = 1e-06
MASKED = -1e30
HIGHEST = lax.Precision.HIGHEST
MESH = pl.DeviceIdType.MESH
ANY = pl.BlockSpec(memory_space=pl.ANY)
VMEM = pl.BlockSpec(memory_space=pltpu.VMEM)


def bucket_onehot(length, buckets, max_distance):
    halfway = buckets // 2
    exact_max = halfway // 2
    relative_list = list(range(-(length - 1), length))
    beyond_list = [
        min(
            halfway - 1,
            exact_max
            + math.floor(
                math.log(max(abs(shift), 1) / exact_max)
                / math.log(max_distance / exact_max)
                * (halfway - exact_max)
            ),
        )
        for shift in relative_list
    ]
    relative = np.array(relative_list)
    beyond = np.array(beyond_list)
    distance = np.abs(relative)
    bucket_ids = np.where(relative > 0, halfway, 0) + np.where(
        distance < exact_max, distance, beyond
    )
    return (bucket_ids[None, :] == np.arange(buckets)[:, None]).astype(np.float32)


def place():
    psg = lax.axis_index("psg")
    mp = lax.axis_index("mp")
    return psg // 8, (psg // 4) % 2, psg % 4, mp // 2, mp % 2


def psg_of(x, yl, z):
    return x * 8 + yl * 4 + z


def remote(src, dst, send_sem, recv_sem, device):
    return pltpu.make_async_remote_copy(
        src_ref=src,
        dst_ref=dst,
        send_sem=send_sem,
        recv_sem=recv_sem,
        device_id=device,
        device_id_type=MESH,
    )


def signal(device):
    pl.semaphore_signal(
        pltpu.get_barrier_semaphore(), inc=1, device_id=device, device_id_type=MESH
    )


def psg_gather_kernel(src, out, send_sem, recv_sem, own_sem):
    me = lax.axis_index("psg")
    mp = lax.axis_index("mp")

    def greet(k, c):
        signal((lax.rem(me + k, NPSG), mp))
        return c

    lax.fori_loop(1, NPSG, greet, 0)
    own = pltpu.make_async_copy(src, out.at[me], own_sem)
    own.start()
    pl.semaphore_wait(pltpu.get_barrier_semaphore(), NPSG - 1)

    def copy(k):
        return remote(
            src, out.at[me], send_sem.at[k], recv_sem.at[k], (lax.rem(me + k, NPSG), mp)
        )

    def start(k, c):
        copy(k).start()
        return c

    lax.fori_loop(1, NPSG, start, 0)

    def finish(k, c):
        copy(k).wait()
        return c

    lax.fori_loop(1, NPSG, finish, 0)
    own.wait()


def psg_gather(x, collective_id):
    return pl.pallas_call(
        psg_gather_kernel,
        out_shape=jax.ShapeDtypeStruct((NPSG,) + x.shape, x.dtype),
        in_specs=[VMEM],
        out_specs=VMEM,
        scratch_shapes=[
            pltpu.SemaphoreType.DMA((NPSG,)),
            pltpu.SemaphoreType.DMA((NPSG,)),
            pltpu.SemaphoreType.DMA,
        ],
        compiler_params=pltpu.CompilerParams(
            collective_id=collective_id, has_side_effects=True
        ),
    )(x)


def mp_exchange_kernel(split, src, out, send_sem, recv_sem, own_sem):
    psg = lax.axis_index("psg")
    me = lax.axis_index("mp")
    for k in range(1, NMP):
        signal((psg, lax.rem(me + k, NMP)))
    own = pltpu.make_async_copy(src.at[me] if split else src, out.at[me], own_sem)
    own.start()
    pl.semaphore_wait(pltpu.get_barrier_semaphore(), NMP - 1)
    copies = []
    for k in range(1, NMP):
        to = lax.rem(me + k, NMP)
        copies.append(
            remote(
                src.at[to] if split else src,
                out.at[me],
                send_sem.at[k],
                recv_sem.at[k],
                (psg, to),
            )
        )
        copies[-1].start()
    for copy in copies:
        copy.wait()
    own.wait()


def mp_exchange(x, collective_id, split):
    shape = x.shape if split else (NMP,) + x.shape
    return pl.pallas_call(
        functools.partial(mp_exchange_kernel, split),
        out_shape=jax.ShapeDtypeStruct(shape, x.dtype),
        in_specs=[VMEM],
        out_specs=VMEM,
        scratch_shapes=[
            pltpu.SemaphoreType.DMA((NMP,)),
            pltpu.SemaphoreType.DMA((NMP,)),
            pltpu.SemaphoreType.DMA,
        ],
        compiler_params=pltpu.CompilerParams(
            collective_id=collective_id, has_side_effects=True
        ),
    )(x)


def spread_kernel(src, out, send_sem, recv_sem, own_sem):
    psg = lax.axis_index("psg")
    mp = lax.axis_index("mp")
    x = psg // 8
    mine = x == mp

    def greet(k, c):
        frm = lax.rem(psg + k, NPSG)

        @pl.when(jnp.logical_or(k > 0, jnp.logical_not(mine)))
        def _():
            signal((frm, x))

        return c

    lax.fori_loop(0, NPSG, greet, 0)
    first = lax.rem(psg, 8) * 4 + mp

    def copy(k):
        t = lax.rem(first + k, NPSG)
        c, m = t // 4, lax.rem(t, 4)
        return remote(src.at[c, m], out.at[psg], send_sem.at[k], recv_sem.at[psg], (mp * 8 + c, m))

    @pl.when(mine)
    def _():
        own = pltpu.make_async_copy(src.at[lax.rem(psg, 8), mp], out.at[psg], own_sem)
        own.start()
        own.wait()
        pl.semaphore_wait(pltpu.get_barrier_semaphore(), NPSG - 1)

    @pl.when(jnp.logical_not(mine))
    def _():
        pl.semaphore_wait(pltpu.get_barrier_semaphore(), NPSG)
        copy(0).start()

    def start(k, c):
        copy(k).start()
        return c

    lax.fori_loop(1, NPSG, start, 0)

    def arrived(k, c):
        frm = lax.rem(psg + k, NPSG)
        remote(src.at[0, 0], out.at[frm], send_sem.at[0], recv_sem.at[frm], (frm, x)).wait_recv()
        return c

    def sent(k, c):
        copy(k).wait_send()
        return c

    @pl.when(jnp.logical_not(mine))
    def _():
        arrived(0, 0)
        copy(0).wait_send()

    lax.fori_loop(1, NPSG, arrived, 0)
    lax.fori_loop(1, NPSG, sent, 0)


def spread(x, collective_id):
    return pl.pallas_call(
        spread_kernel,
        out_shape=jax.ShapeDtypeStruct((NPSG,) + x.shape[2:], x.dtype),
        in_specs=[VMEM],
        out_specs=VMEM,
        scratch_shapes=[
            pltpu.SemaphoreType.DMA((NPSG,)),
            pltpu.SemaphoreType.DMA((NPSG,)),
            pltpu.SemaphoreType.DMA,
        ],
        compiler_params=pltpu.CompilerParams(
            collective_id=collective_id, has_side_effects=True
        ),
    )(x)


def lookup_kernel(ids, base, table, out, rows, sems):
    copies = []
    held = []
    for i in range(CLAIMS * POS):
        local = ids[i] - base[0]
        inside = jnp.logical_and(local >= 0, local < table.shape[0])
        local = jnp.clip(local, 0, table.shape[0] - 1)
        start = pl.multiple_of((local // 16) * 16, 16)
        held.append(jnp.where(inside, local - start, -1))
        copies.append(
            pltpu.make_async_copy(table.at[pl.ds(start, 16), :], rows.at[i], sems.at[i])
        )
        copies[-1].start()
    at = lax.broadcasted_iota(jnp.int32, (16, 128), 0)
    for i in range(CLAIMS * POS):
        copies[i].wait()
        picked = jnp.where(at == held[i], rows[i].astype(jnp.float32), 0.0)
        out[pl.ds(i, 1), :] = jnp.sum(picked, axis=0, keepdims=True)


def lookup(ids, base, table):
    smem = pl.BlockSpec(memory_space=pltpu.SMEM)
    return pl.pallas_call(
        lookup_kernel,
        out_shape=jax.ShapeDtypeStruct((CLAIMS * POS, 128), jnp.float32),
        in_specs=[smem, smem, ANY],
        out_specs=VMEM,
        scratch_shapes=[
            pltpu.VMEM((CLAIMS * POS, 16, 128), jnp.bfloat16),
            pltpu.SemaphoreType.DMA((CLAIMS * POS,)),
        ],
    )(ids, base, table)


def split3(values):
    high = values.astype(jnp.bfloat16)
    rest = values - high.astype(jnp.float32)
    middle = rest.astype(jnp.bfloat16)
    low = (rest - middle.astype(jnp.float32)).astype(jnp.bfloat16)
    return jnp.concatenate([high, middle, low], axis=0)


def dot3(values, weights, contract=0):
    n = values.shape[0]
    parts = lax.dot_general(
        split3(values),
        weights,
        (((1,), (contract,)), ((), ())),
        preferred_element_type=jnp.float32,
    )
    return parts[:n] + parts[n : 2 * n] + parts[2 * n :]


ALL = slice(None)


def encoder_kernel(
    tokens,
    enc_gain,
    w_ref,
    bias_in,
    onehot,
    mask_add,
    enc_output,
    final_gain,
    found,
    dec_gain,
    cross_query,
    cross_keyval,
    enc_out,
    u_out,
    emb_out,
    g_ref,
    normed,
    acc,
    qkv,
    e_ref,
    att,
    transit,
    bias,
    tok_here,
    block,
    mp_buf,
    x_buf,
    yz_buf,
    send_sem,
    recv_sem,
    own_sem,
):
    f32 = jnp.float32
    bf16 = jnp.bfloat16
    x, yl, z, yh, core = place()
    psg = lax.axis_index("psg")
    mp = lax.axis_index("mp")
    y = yh * 2 + yl
    y_dev = (psg_of(x, 1 - yl, z), mp)

    def dev(axis, step):
        if axis == "x":
            return (psg_of(lax.rem(x + step, 4), yl, z), mp)
        return (psg_of(x, yl, lax.rem(z + step, 4)), mp)

    def yz_dev(k):
        t = lax.rem(yl * 4 + z + k, 8)
        return (x * 8 + t, mp)

    def mp_dev(k):
        return (psg, lax.rem(mp + k, NMP))

    def y_step(step):
        t = lax.rem(y + step, 4)
        return (psg_of(x, lax.rem(t, 2), z), (t // 2) * 2 + core)

    other_core = (psg, yh * 2 + 1 - core)
    same_half = (x // 2) == yh
    yl_to = jnp.where(same_half, yl, 1 - yl)

    def block_to(k):
        return (psg_of(lax.rem(x + k, 4), yl_to, z), x)

    mine = x == mp

    load_tokens = pltpu.make_async_copy(tokens, normed, own_sem.at[0])
    load_tokens.start()
    own = pltpu.make_async_copy(
        w_ref, g_ref.at[:, x, z, pl.ds(pl.multiple_of(yl * 128, 128), 128), :], own_sem.at[1]
    )
    own.start()
    load_here = pltpu.make_async_copy(
        tokens.at[:, pl.ds(pl.multiple_of(mp * 1024, 128), 1024)], tok_here, own_sem.at[2]
    )
    load_here.start()
    load_block = pltpu.make_async_copy(enc_output, block.at[pl.ds(0, 512)], own_sem.at[3])
    load_block.start()

    for k in range(1, 4):
        signal(dev("x", k))
        signal(mp_dev(k))
    for k in range(1, 8):
        signal(yz_dev(k))
    signal(y_step(1))
    signal(y_step(3))
    for m in range(NMP):
        frm = psg_of(mp, jnp.where((m // 2) == yh, yl, 1 - yl), z)

        @pl.when(jnp.logical_not(jnp.logical_and(mine, m == mp)))
        def _():
            signal((frm, m))

    def g(k, xs, zs, yls, cols=None):
        rows = ALL if yls is None else pl.ds(pl.multiple_of(yls * 128, 128), 128)
        c = ALL if cols is None else pl.ds(cols[0], cols[1])
        return g_ref.at[k, xs, zs, rows, c]

    def wide(c):
        return None if c is None else (c * 256, 256)

    def low_cols(c):
        return (0, 256) if c is None else (c * 128, 128)

    def high_cols(c):
        return (256, 256) if c is None else (256 + c * 128, 128)

    sent = []

    def send(t, src, dst, device):
        copy = remote(src, dst, send_sem.at[t], recv_sem.at[t], device)
        copy.start()
        sent.append(copy)
        return copy

    class Ring:
        def __init__(self, t, axis, piece, first=None):
            self.t, self.axis, self.piece = t, axis, piece
            self.at = x if axis == "x" else z
            src = piece(self.at) if first is None else first
            self.up = send(t, src, piece(self.at), dev(axis, 1))
            self.down = send(t + 1, src, piece(self.at), dev(axis, 3))

        def forward(self):
            below = lax.rem(self.at + 3, 4)
            above = lax.rem(self.at + 1, 4)
            self.up.wait_recv()
            up = self.piece(below, 0)
            self.f_up = send(self.t + 2, up, up, dev(self.axis, 1))
            self.down.wait_recv()
            down = self.piece(above, 1)
            self.f_down = send(self.t + 3, down, down, dev(self.axis, 3))

        def end(self):
            self.f_up.wait_recv()
            self.f_down.wait_recv()

    pl.semaphore_wait(pltpu.get_barrier_semaphore(), jnp.where(mine, 18, 19))

    yd = send(0, w_ref.at[0], g(0, x, z, yl), y_dev)
    ye = send(1, w_ref.at[1], g(1, x, z, yl), y_dev)
    a1 = Ring(
        4, "x", lambda v, c=None: g(2, v, z, yl, low_cols(c)), w_ref.at[2, :, pl.ds(0, 256)]
    )
    b1 = Ring(
        8, "z", lambda v, c=None: g(2, x, v, yl, high_cols(c)), w_ref.at[2, :, pl.ds(256, 256)]
    )
    mp_buf[mp] = found[...]
    mps = [send(52 + k, found, mp_buf.at[mp], mp_dev(k)) for k in range(1, 4)]
    own.wait()
    yd.wait_recv()
    d2 = Ring(20, "x", lambda v, c=None: g(0, v, z, None, wide(c)))
    ye.wait_recv()
    e2 = Ring(24, "z", lambda v, c=None: g(1, x, v, None, wide(c)))
    a1.forward()
    b1.forward()

    for copy in mps:
        copy.wait_recv()
    emb = mp_buf[0] + mp_buf[1] + mp_buf[2] + mp_buf[3]
    emb_out[...] = emb
    terms = dot3(emb * dec_gain[...], cross_query[...])
    squares = jnp.sum(emb * emb, axis=1, keepdims=True)
    x_buf[x, :, pl.ds(0, 512)] = terms
    x_buf[x, :, pl.ds(512, 128)] = jnp.broadcast_to(squares, (8, 128))
    xs = [send(56 + k, x_buf.at[x], x_buf.at[x], dev("x", k)) for k in range(1, 4)]

    a1.end()
    a2 = Ring(12, "z", lambda v, c=None: g(2, ALL, v, yl, low_cols(c)))
    b1.end()
    b2 = Ring(16, "x", lambda v, c=None: g(2, v, ALL, yl, high_cols(c)))

    load_tokens.wait()

    def norm_rows(first, count):
        def body(i, c):
            rows = pl.ds(pl.multiple_of(i * 16, 16), 16)
            values = normed[rows, :].astype(f32)
            mean = jnp.sum(values * values, axis=1, keepdims=True) / D
            inverse = lax.rsqrt(mean + EPSILON)
            scaled = (values * inverse * enc_gain[...]).astype(bf16)
            for p in range(NPSG):
                to = ((p // 8) * 4 + p % 4) * 2 + (p // 4) % 2
                normed[rows, pl.ds(to * 128, 128)] = scaled[:, p * 128 : (p + 1) * 128]
            return c

        lax.fori_loop(first, first + count, body, 0)

    norm_rows(0, 24)

    for copy in xs:
        copy.wait_recv()
    yz = yl * 4 + z
    yz_buf[yz] = x_buf[0] + x_buf[1] + x_buf[2] + x_buf[3]
    yzs = [send(60 + k, yz_buf.at[yz], yz_buf.at[yz], yz_dev(k)) for k in range(1, 8)]

    d2.forward()
    e2.forward()
    norm_rows(24, 20)
    d2.end()
    d3 = Ring(28, "z", lambda v, c=None: g(0, ALL, v, None, wide(c)))
    e2.end()
    e3 = Ring(32, "x", lambda v, c=None: g(1, v, ALL, None, wide(c)))
    a2.forward()
    b2.forward()
    norm_rows(44, 20)

    for copy in yzs:
        copy.wait_recv()
    joined = yz_buf[0]
    for k in range(1, 8):
        joined = joined + yz_buf[k]
    cquery = joined[:, :512] * lax.rsqrt(joined[:, 512:513] / D + EPSILON)
    spread_q = jnp.broadcast_to(cquery[:, None, :], (8, 8, 512)).reshape(64, 512)
    head_of_row = lax.rem(lax.broadcasted_iota(jnp.int32, (64, 512), 0), 8)
    head_of_lane = lax.broadcasted_iota(jnp.int32, (64, 512), 1) // HEAD_DIM
    spread_q = jnp.where(head_of_row == head_of_lane, spread_q, 0.0)
    folded = dot3(spread_q, cross_keyval[0], 1)
    folded = folded * final_gain[:, pl.ds(pl.multiple_of(psg * 128, 128), 128)]
    high = folded.astype(bf16)
    load_block.wait()
    block[pl.ds(512, 64), :] = high
    block[pl.ds(576, 64), :] = (folded - high.astype(f32)).astype(bf16)

    def e(ms, yls, zs):
        col = pl.multiple_of((yls * 4 + zs) * 128, 128)
        return e_ref.at[ms, :, pl.ds(col, 128)]

    def block_copy(k):
        return remote(block, e(mp, yl, z), send_sem.at[36 + k], recv_sem.at[40 + mp], block_to(k))

    keep = pltpu.make_async_copy(block, e(mp, yl, z), own_sem.at[4])

    @pl.when(mine)
    def _():
        keep.start()

    @pl.when(jnp.logical_not(mine))
    def _():
        block_copy(0).start()

    for k in range(1, 4):
        block_copy(k).start()

    a2.end()
    low = g(2, ALL, ALL, yl, low_cols(None))
    ya = send(2, low, low, y_dev)
    b2.end()
    hi = g(2, ALL, ALL, yl, high_cols(None))
    yb = send(3, hi, hi, y_dev)

    table = dot3(bias_in[...], onehot[...])
    for h in range(8):
        row = jnp.broadcast_to(table[h : h + 1], (SEQ, 512))
        bias[h] = pltpu.roll(row, 0, 1, stride=1, stride_axis=0)[:, :SEQ]

    for m in range(NMP):
        got = remote(block, e(m, yl, z), send_sem.at[36], recv_sem.at[40 + m], y_dev)
        pl.when(jnp.logical_not(jnp.logical_and(mine, m == mp)))(got.wait_recv)

    @pl.when(mine)
    def _():
        keep.wait()

    near = pl.ds(yh * 2, 2)
    far_half = pl.ds(2 - yh * 2, 2)
    y1 = send(44, e(near, yl, z), e(near, yl, z), y_dev)
    y2 = send(45, e(far_half, 1 - yl, z), e(far_half, 1 - yl, z), y_dev)

    d3.forward()
    e3.forward()

    def product(k, rows, xi, zi):
        at = pl.multiple_of((xi * 4 + zi) * 256, 256)
        return jnp.dot(
            normed[rows, pl.ds(at, 256)], g_ref[k, xi, zi], preferred_element_type=f32
        )

    def project(step):
        def body(i, c):
            step(pl.ds(pl.multiple_of(i * 256, 256), 256))
            return c

        lax.fori_loop(0, 4, body, 0)

    def first_q(rows):
        total = None
        for xi in range(4):
            for dz in (0, 1, 3):
                term = product(0, rows, xi, lax.rem(z + dz, 4))
                total = term if total is None else total + term
        acc[0, rows, :] = total

    def first_k(rows):
        total = None
        for zi in range(4):
            for dx in (0, 1, 3):
                term = product(1, rows, lax.rem(x + dx, 4), zi)
                total = term if total is None else total + term
        acc[1, rows, :] = total

    def all_v(rows):
        total = None
        for xi in range(4):
            for zi in range(4):
                term = product(2, rows, xi, zi)
                total = term if total is None else total + term
        qkv[2, rows, :] = total.astype(bf16)

    def last_q(rows):
        total = acc[0, rows, :]
        for xi in range(4):
            total = total + product(0, rows, xi, lax.rem(z + 2, 4))
        qkv[0, rows, :] = total.astype(bf16)

    def last_k(rows):
        total = acc[1, rows, :]
        for zi in range(4):
            total = total + product(1, rows, lax.rem(x + 2, 4), zi)
        qkv[1, rows, :] = total.astype(bf16)

    project(first_q)
    y1.wait_recv()
    y2.wait_recv()
    e_up = [send(46 + i, e(ALL, i, z), e(ALL, i, z), dev("z", 1)) for i in range(2)]
    e_down = [send(48 + i, e(ALL, i, z), e(ALL, i, z), dev("z", 3)) for i in (1, 0)]
    project(first_k)
    ya.wait_recv()
    yb.wait_recv()
    project(all_v)
    d3.end()
    project(last_q)
    e3.end()
    project(last_k)

    lane = lax.broadcasted_iota(jnp.int32, (SEQ, 128), 1)

    def attend(p):
        rows = pl.ds(p * SEQ, SEQ)

        def body(j, c):
            lanes = pl.ds(pl.multiple_of(j * 128, 128), 128)
            q2 = qkv[0, rows, lanes]
            k2 = qkv[1, rows, lanes]
            v2 = qkv[2, rows, lanes]
            outs = []
            for t in range(2):
                qt = jnp.where((lane // HEAD_DIM) == t, q2, jnp.zeros_like(q2))
                s = lax.dot_general(
                    qt, k2, (((1,), (1,)), ((), ())), preferred_element_type=f32
                )
                s = s + bias[2 * j + t] + mask_add[pl.ds(p, 1), :]
                wts = jnp.exp(s - jnp.max(s, axis=1, keepdims=True))
                scale = 1.0 / jnp.sum(wts, axis=1, keepdims=True)
                outs.append(
                    jnp.dot((wts * scale).astype(bf16), v2, preferred_element_type=f32)
                )
            att[mp, rows, lanes] = jnp.where(lane < HEAD_DIM, outs[0], outs[1]).astype(bf16)
            return c

        lax.fori_loop(0, 4, body, 0)

    hops, ends, cores, lasts = [], [], [], []
    far = (1 - yh) * 2 + core

    def hand_out(p):
        rows = pl.ds(p * SEQ, SEQ)
        cores.append(send(68 + p, att.at[mp, rows], att.at[mp, rows], other_core))
        hops.append(
            send(72 + p, att.at[mp, rows], transit.at[p], y_step(1 if p % 2 == 0 else 3))
        )

    def hand_on(p):
        rows = pl.ds(p * SEQ, SEQ)
        hops[p].wait_recv()
        frm = lax.rem(y + (3 if p % 2 == 0 else 1), 4)
        slot = (frm // 2) * 2 + core
        ends.append(
            send(76 + p, transit.at[p], att.at[slot, rows], y_step(1 if p % 2 == 0 else 3))
        )

    def hand_over(p):
        rows = pl.ds(p * SEQ, SEQ)
        ends[p].wait_recv()
        lasts.append(send(80 + p, att.at[far, rows], att.at[far, rows], other_core))

    attend(0)
    hand_out(0)
    attend(1)
    hand_out(1)
    hand_on(0)
    e_up[0].wait_recv()
    piece = e(ALL, 0, lax.rem(z + 3, 4))
    ef_up = send(50, piece, piece, dev("z", 1))
    e_down[0].wait_recv()
    piece = e(ALL, 1, lax.rem(z + 1, 4))
    ef_down = send(51, piece, piece, dev("z", 3))
    attend(2)
    hand_out(2)
    hand_on(1)
    hand_over(0)
    attend(3)
    hand_out(3)
    hand_on(2)
    hand_over(1)
    hand_on(3)
    load_here.wait()
    e_up[1].wait_recv()
    e_down[1].wait_recv()
    ef_up.wait_recv()
    ef_down.wait_recv()
    hand_over(2)
    hand_over(3)
    u_copy = pltpu.make_async_copy(e_ref.at[:, pl.ds(512, 128), :], u_out, own_sem.at[5])
    u_copy.start()
    for p in range(4):
        cores[p].wait_recv()
        lasts[p].wait_recv()
        rows = pl.ds(p * SEQ, SEQ)

        def out_cols(i, c):
            cols = pl.ds(pl.multiple_of(i * 512, 512), 512)
            total = None
            for m in range(NMP):
                term = jnp.dot(
                    att[m, rows, :], e_ref[m, pl.ds(0, 512), cols], preferred_element_type=f32
                ).astype(bf16).astype(f32)
                total = term if total is None else total + term
            enc_out[rows, cols] = (tok_here[rows, cols].astype(f32) + total).astype(bf16)
            return c

        lax.fori_loop(0, 2, out_cols, 0)

    u_copy.wait()
    for copy in sent:
        copy.wait_send()
    for k in range(1, 4):
        block_copy(k).wait_send()

    @pl.when(jnp.logical_not(mine))
    def _():
        block_copy(0).wait_send()


def encoder(args):
    tok_rows = args[0].shape[0]
    bf16 = jnp.bfloat16
    return pl.pallas_call(
        encoder_kernel,
        out_shape=(
            jax.ShapeDtypeStruct((tok_rows, 1024), bf16),
            jax.ShapeDtypeStruct((NMP, 128, 1024), bf16),
            jax.ShapeDtypeStruct((CLAIMS * POS, 128), jnp.float32),
        ),
        in_specs=[ANY, VMEM, ANY, VMEM, VMEM, VMEM, ANY] + [VMEM] * 5,
        out_specs=(VMEM, ANY, VMEM),
        scratch_shapes=[
            pltpu.VMEM((3, 4, 4, 256, 512), bf16),
            pltpu.VMEM((tok_rows, D), bf16),
            pltpu.VMEM((2, tok_rows, 512), jnp.float32),
            pltpu.VMEM((3, tok_rows, 512), bf16),
            pltpu.VMEM((NMP, 640, 1024), bf16),
            pltpu.VMEM((NMP, tok_rows, 512), bf16),
            pltpu.VMEM((4, SEQ, 512), bf16),
            pltpu.VMEM((8, SEQ, SEQ), jnp.float32),
            pltpu.VMEM((tok_rows, 1024), bf16),
            pltpu.VMEM((640, 128), bf16),
            pltpu.VMEM((NMP, 8, 128), jnp.float32),
            pltpu.VMEM((4, 8, 640), jnp.float32),
            pltpu.VMEM((8, 8, 640), jnp.float32),
            pltpu.SemaphoreType.DMA((84,)),
            pltpu.SemaphoreType.DMA((84,)),
            pltpu.SemaphoreType.DMA((6,)),
        ],
        compiler_params=pltpu.CompilerParams(
            collective_id=1, has_side_effects=True, vmem_limit_bytes=58 << 20
        ),
    )(*args)


def high_low(values):
    high = values.astype(jnp.bfloat16)
    low = (values - high.astype(jnp.float32)).astype(jnp.bfloat16)
    return high, low


def shards(
    tokens,
    lengths,
    assignment,
    retrieval,
    enc_gain,
    enc_qkv,
    position_bias,
    enc_output,
    final_gain,
    embedding,
    dec_tokens,
    dec_gain,
    cross_query,
    cross_keyval,
    cross_output,
):
    f32 = jnp.float32
    psg = lax.axis_index("psg")
    mp = lax.axis_index("mp")
    tok_rows = tokens.shape[0]
    passages_here = lengths.shape[0]
    heads_here = enc_qkv.shape[2] // HEAD_DIM
    query_rows = CLAIMS * POS
    positions = jnp.arange(SEQ)

    vocab_here = embedding.shape[0]
    found = lookup(dec_tokens.reshape(-1), (mp * vocab_here).reshape(1), embedding)
    onehot = bucket_onehot(SEQ, BUCKETS, MAXDIST)
    onehot = np.concatenate([onehot[:, 255:], np.zeros((BUCKETS, 1)), onehot[:, :255]], axis=1)
    mask_add = jnp.where(positions[None, :] < lengths[:, None], 0.0, MASKED)
    encoded, u_all, embedded = encoder(
        (
            tokens,
            enc_gain.reshape(1, D),
            enc_qkv,
            position_bias,
            jnp.asarray(onehot, jnp.bfloat16),
            mask_add,
            enc_output,
            final_gain.reshape(1, D),
            found,
            dec_gain.reshape(1, 128),
            cross_query,
            cross_keyval,
        )
    )
    width = encoded.shape[1]
    gain_here = lax.dynamic_slice_in_dim(final_gain, psg * 128, 128, 0)
    encoded_f = encoded.astype(f32)
    squares = jnp.sum(encoded_f * encoded_f, axis=1).reshape(passages_here, SEQ)

    rows_u = u_all.reshape(NMP, 2, CLAIMS, POS * heads_here, width)
    claim_u = jnp.stack(
        [lax.dynamic_index_in_dim(rows_u, assignment[i], 2, False) for i in range(passages_here)],
        axis=2,
    )
    per_psg = encoded.reshape(passages_here, SEQ, width)
    partial = jnp.einsum("mapnd,pkd->mapnk", claim_u, per_psg, preferred_element_type=f32)
    partial = (partial[:, 0] + partial[:, 1]).reshape(NMP, passages_here * POS * heads_here, SEQ)
    extra = jnp.broadcast_to(
        jnp.concatenate([squares, jnp.zeros_like(squares)], axis=0)[None],
        (NMP, 2 * passages_here, SEQ),
    )
    raw = jnp.sum(mp_exchange(jnp.concatenate([partial, extra], axis=1), 5, True), axis=0)
    n_rows = passages_here * POS * heads_here
    inverse = lax.rsqrt(raw[n_rows : n_rows + passages_here] / D + EPSILON)
    cross = raw[:n_rows].reshape(passages_here, POS * heads_here, SEQ)
    cross = cross * inverse[:, None, :] + retrieval[:, None, None]
    usable = (positions[None, :] < lengths[:, None])[:, None, :]
    masked = jnp.where(usable, cross, MASKED)
    onehot = assignment[None, :] == jnp.arange(CLAIMS)[:, None]
    psg_max = jnp.max(masked, axis=-1)
    local_max = jnp.max(jnp.where(onehot[:, :, None], psg_max[None], MASKED), axis=1)
    chosen_max = jnp.max(jnp.where(onehot[:, :, None], local_max[:, None], MASKED), axis=0)
    weights_c = jnp.where(
        usable, jnp.exp(masked - chosen_max[:, :, None]), 0.0
    )
    local_total = jnp.sum(
        jnp.where(onehot[:, :, None], jnp.sum(weights_c, axis=-1)[None], 0.0), axis=1
    )
    stats = jnp.stack([local_max.reshape(-1), local_total.reshape(-1)])
    stats = jnp.pad(stats, ((0, 6), (0, SEQ - stats.shape[1])))
    sent = jnp.concatenate(
        [(weights_c * inverse[:, None, :]).reshape(n_rows, SEQ), stats], axis=0
    )
    all_w = mp_exchange(sent, 6, False)
    spread_w = jnp.where(
        onehot[None, :, :, None, None],
        all_w[:, :n_rows].reshape(NMP, 1, passages_here, POS * heads_here, SEQ),
        0.0,
    )
    w_high, w_low = high_low(spread_w)
    weighted = jnp.einsum(
        "mcpnk,pkd->mcnd", w_high, per_psg, preferred_element_type=f32
    ) + jnp.einsum("mcpnk,pkd->mcnd", w_low, per_psg, preferred_element_type=f32)
    weighted = weighted.reshape(NMP, query_rows * heads_here, 8, 128).transpose(2, 0, 1, 3)
    both = jnp.concatenate([all_w[:, n_rows, :64], all_w[:, n_rows + 1, :64]], axis=1)
    both = jnp.broadcast_to(
        jnp.pad(both[:, None, :], ((0, 0), (0, 7), (0, 0)))[None], (8, NMP, 8, 128)
    )
    got = spread(jnp.concatenate([weighted, both], axis=2), 7)
    each_max = got[:, 64, :64]
    each_total = got[:, 64, 64:]
    joint_max = jnp.max(each_max, axis=0)
    scale = jnp.exp(each_max - joint_max[None])
    total = jnp.sum(scale * each_total, axis=0)
    mean_rows = jnp.sum(got[:, :64] * scale[:, :, None], axis=0) / total[:, None] * gain_here
    attn_part = jnp.einsum(
        "rhc,chd->rhd",
        mean_rows.reshape(query_rows, heads_here, 128),
        cross_keyval[1].astype(f32).reshape(128, heads_here, HEAD_DIM),
        precision=HIGHEST,
    ).reshape(query_rows, 512)
    cross_attn = jnp.sum(psg_gather(attn_part, 8), axis=0)
    out_part = jnp.dot(cross_attn, cross_output.astype(f32), precision=HIGHEST)
    out_sum = jnp.sum(mp_exchange(out_part, 9, False), axis=0) + embedded
    decoded = lax.dynamic_slice_in_dim(out_sum, mp * 32, 32, 1)
    return (encoded, decoded.astype(jnp.bfloat16).reshape(CLAIMS, POS, 32))


def solution(mesh):
    in_specs = (
        P("psg", None),
        P("psg"),
        P("psg"),
        P("psg"),
        P(),
        P(None, "psg", "mp"),
        P("mp", None),
        P("mp", "psg"),
        P(),
        P("mp", "psg"),
        P(),
        P("psg"),
        P("psg", "mp"),
        P(None, "psg", "mp"),
        P("mp", "psg"),
    )
    out_specs = (P("psg", "mp"), P(None, None, ("psg", "mp")))
    return jax.shard_map(shards, mesh=mesh, in_specs=in_specs, out_specs=out_specs, check_vma=False)
```

time: 412 us -> 286 us (0.69)
  matrix products: 47.7 us -> 3.39 us
  other arithmetic: 31.9 us -> 9.01 us
  local copies, waits for them, and re-layouts: 33.6 us -> 12.3 us
  Pallas kernels: 273 us -> 252 us
  between operations: 23.8 us -> 8.56 us
    dot_general x10 -> x0, matrix products: 44.4 us -> none  [the longest x4 17.6 us: shards(): jnp.dot(groups[m], blocks[m, :512], preferred_element_type=f32)]
    pallas_call x2 -> x1, Pallas kernels: 30.5 us -> 13.4 us  [psg_gather(): pl.pallas_call(psg_gather_kernel, out_shape=jax.ShapeDtypeStruct((NPSG,)...]
    sub x1 -> x0, other arithmetic: 12.3 us -> none  [shards(): weights = jnp.exp(scores - jnp.max(scores, axis=-1, keepdims=True))]
    reshape x4 -> x1, local copies, waits for them, and re-layouts: 10.5 us -> 0.6 us  [shards(): dec_tokens.reshape(-1)]
    slice x10 -> x0, local copies, waits for them, and re-layouts: 9.25 us -> none  [the longest x3 3.39 us: toeplitz(): return repeated.reshape(heads_count, length, 2 * length - 1)[:, :, :length]]
    reduce_sum x4 -> x1, other arithmetic: 7.21 us -> 0.48 us  [shards(): squares = jnp.sum(encoded_f * encoded_f, axis=1).reshape(passages_here, SEQ)]
    pallas_call x4 -> x3, Pallas kernels: 32.9 us -> 29.1 us  [mp_exchange(): pl.pallas_call(functools.partial(mp_exchange_kernel, split), out_shape=ja...]
where the time goes in v2:
time: 286 us; the launch traced here: 285 us
  Pallas kernels  252 us (88%)
  local copies, waits for them, and re-layouts  12.3 us (4%)
  other arithmetic  9.01 us (3%)
  between operations  8.56 us (3%)
  matrix products  3.39 us (1%)
    pallas_call x1, Pallas kernels, encoder(): pl.pallas_call(encoder_kernel, out_shape=(jax.ShapeDtypeStruct((tok_rows,...  171 us
    pallas_call x1, Pallas kernels, spread(): pl.pallas_call(spread_kernel, out_shape=jax.ShapeDtypeStruct((NPSG,) + x....  36.1 us
    pallas_call x3, Pallas kernels, mp_exchange(): pl.pallas_call(functools.partial(mp_exchange_kernel, split), out_shape=ja...  29.1 us
    pallas_call x1, Pallas kernels, psg_gather(): pl.pallas_call(psg_gather_kernel, out_shape=jax.ShapeDtypeStruct((NPSG,)...  13.4 us

profile of v2, /device:TPU:1, one launch (start us, length us, event | category | flops | bytes accessed | tf_op | source)
XLA Modules:
  0.0 285.3 jit_solution(9473347189679764738)
XLA Ops:
  0.7 1.5 fusion.28
  9.8 0.8 copy.43
  11.1 2.2 shard_map.167.found
  14.0 171.3 %shard_map.168 = (bf16[1024,1024]{1,0:T(8,128)(2,1)}, bf16[4,128,1024]{2,1,0:T(8,128)(2,1)}, f32[8,128]{1,0:T(8,128)}) custom-call(bf16[1024,4096]{1,0:T(8,128)(2,1)} %tokens.1, f32[1,4096]{1,0:T(1,128)} %bitcast.109, bf16[3,128,512]{2,1,0:T(8,128)(2,1)} %w_ref.1, f32[8,32]{1,0:T(8,128)} %bias_in.1, bf16[32,512]{1,0:T(8,128)(2,1)} %constant.45.clone.onehot, ...), custom_call_target="tpu_custom_call" | custom-call | tf_op jit(solution)/shard_map/pallas_call | solution.py:753
  185.3 1.4 dynamic-slice_bitcast_fusion.3
  187.2 0.8 convolution_bitcast_fusion.2
  188.7 0.7 pad_maximum_fusion.1.src
  189.4 12.3 %shard_map.169 = f32[4,72,256]{2,1,0:T(8,128)} custom-call(f32[4,72,256]{2,1,0:T(8,128)} %pad_maximum_fusion.1.src), custom_call_target="tpu_custom_call" | custom-call | tf_op jit(solution)/shard_map/pallas_call | solution.py:158
  201.7 1.0 reduce_sum.75
  204.7 8.8 %shard_map.170 = f32[4,72,256]{2,1,0:T(8,128)} custom-call(f32[72,256]{1,0:T(8,128)} %pad_maximum_fusion.2.src), custom_call_target="tpu_custom_call" | custom-call | tf_op jit(solution)/shard_map/pallas_call | solution.py:158
  213.5 1.0 slice.53
  214.5 0.7 convolution_bitcast_fusion
  215.2 0.7 fusion
  216.4 0.8 fusion.27
  217.3 1.1 pad_maximum_fusion.src
  218.4 36.1 %shard_map.171 = f32[32,72,128]{2,1,0:T(8,128)} custom-call(f32[8,4,72,128]{3,2,1,0:T(8,128)} %pad_maximum_fusion.src), custom_call_target="tpu_custom_call" | custom-call | tf_op jit(solution)/shard_map/pallas_call | solution.py:234
  254.5 1.1 fusion.26
  255.6 1.6 multiply_reduce_fusion.1
  257.3 0.8 dynamic_slice.23
  259.3 13.4 %shard_map.172 = f32[32,8,512]{2,1,0:T(8,128)} custom-call(f32[8,512]{1,0:T(8,128)} %reshape.170.src), custom_call_target="tpu_custom_call" | custom-call | tf_op jit(solution)/shard_map/pallas_call | solution.py:114
  272.7 1.1 reduce_sum.81
  273.8 0.8 fusion.29.src
  274.6 8.0 %shard_map.173 = f32[4,8,128]{2,1,0:T(8,128)} custom-call(f32[8,128]{1,0:T(8,128)} %fusion.29.src), custom_call_target="tpu_custom_call" | custom-call | tf_op jit(solution)/shard_map/pallas_call | solution.py:158
  284.0 1.3 copy.73
  (55 shorter events, 7.5 us)
Async XLA Ops:
  0.6 273.2 %copy-start = (bf16[512,128]{1,0:T(8,128)(2,1)S(1)}, bf16[512,128]{1,0:T(8,128)(2,1)}, u32[]{:S(2)}) copy-start(bf16[512,128]{1,0:T(8,128)(2,1)} %param.30) | copy-start | bytes 393220
  0.6 12.7 %copy-start.5 = (s32[4]{0:T(128)S(1)}, s32[4]{0:T(128)}, u32[]{:S(2)}) copy-start(s32[4]{0:T(128)} %param.17) | copy-start | bytes 52
  185.3 1.9 copy-start.1
  188.1 14.6 %copy-start.4 = (f32[4]{0:T(128)S(1)}, f32[4]{0:T(128)}, u32[]{:S(2)}) copy-start(f32[4]{0:T(128)} %param.19) | copy-start | bytes 52
  188.1 15.1 %copy-start.2 = (s32[4]{0:T(128)S(1)}, s32[4]{0:T(128)}, u32[]{:S(2)}) copy-start(s32[4]{0:T(128)} %param.18) | copy-start | bytes 52
  218.4 39.7 %slice-start = ((bf16[2,128,512]{2,1,0:T(8,128)(2,1)}), bf16[1,128,512]{2,1,0:T(8,128)(2,1)S(1)}, s32[]{:S(2)}) async-start(bf16[2,128,512]{2,1,0:T(8,128)(2,1)} %cross_keyval.1), calls=%async_computation | async-start | bytes 262144 | tf_op jit(solution)/shard_map/slice | solution.py:903
  254.5 28.8 %copy-start.3 = (f32[8,128]{1,0:T(8,128)S(1)}, f32[8,128]{1,0:T(8,128)}, u32[]{:S(2)}) copy-start(f32[8,128]{1,0:T(8,128)} %get-tuple-element.7) | copy-start | bytes 12292

commit v3 on v2

--- a/solution.py
+++ b/solution.py
@@ -20,7 +20,6 @@
 NMP = 4
 EPSILON = 1e-06
 MASKED = -1e30
-HIGHEST = lax.Precision.HIGHEST
 MESH = pl.DeviceIdType.MESH
 ANY = pl.BlockSpec(memory_space=pl.ANY)
 VMEM = pl.BlockSpec(memory_space=pltpu.VMEM)
@@ -78,180 +77,12 @@
     )
 
 
-def psg_gather_kernel(src, out, send_sem, recv_sem, own_sem):
-    me = lax.axis_index("psg")
-    mp = lax.axis_index("mp")
-
-    def greet(k, c):
-        signal((lax.rem(me + k, NPSG), mp))
-        return c
-
-    lax.fori_loop(1, NPSG, greet, 0)
-    own = pltpu.make_async_copy(src, out.at[me], own_sem)
-    own.start()
-    pl.semaphore_wait(pltpu.get_barrier_semaphore(), NPSG - 1)
-
-    def copy(k):
-        return remote(
-            src, out.at[me], send_sem.at[k], recv_sem.at[k], (lax.rem(me + k, NPSG), mp)
-        )
-
-    def start(k, c):
-        copy(k).start()
-        return c
-
-    lax.fori_loop(1, NPSG, start, 0)
-
-    def finish(k, c):
-        copy(k).wait()
-        return c
-
-    lax.fori_loop(1, NPSG, finish, 0)
-    own.wait()
-
-
-def psg_gather(x, collective_id):
-    return pl.pallas_call(
-        psg_gather_kernel,
-        out_shape=jax.ShapeDtypeStruct((NPSG,) + x.shape, x.dtype),
-        in_specs=[VMEM],
-        out_specs=VMEM,
-        scratch_shapes=[
-            pltpu.SemaphoreType.DMA((NPSG,)),
-            pltpu.SemaphoreType.DMA((NPSG,)),
-            pltpu.SemaphoreType.DMA,
-        ],
-        compiler_params=pltpu.CompilerParams(
-            collective_id=collective_id, has_side_effects=True
-        ),
-    )(x)
-
-
-def mp_exchange_kernel(split, src, out, send_sem, recv_sem, own_sem):
-    psg = lax.axis_index("psg")
-    me = lax.axis_index("mp")
-    for k in range(1, NMP):
-        signal((psg, lax.rem(me + k, NMP)))
-    own = pltpu.make_async_copy(src.at[me] if split else src, out.at[me], own_sem)
-    own.start()
-    pl.semaphore_wait(pltpu.get_barrier_semaphore(), NMP - 1)
-    copies = []
-    for k in range(1, NMP):
-        to = lax.rem(me + k, NMP)
-        copies.append(
-            remote(
-                src.at[to] if split else src,
-                out.at[me],
-                send_sem.at[k],
-                recv_sem.at[k],
-                (psg, to),
-            )
-        )
-        copies[-1].start()
-    for copy in copies:
-        copy.wait()
-    own.wait()
-
-
-def mp_exchange(x, collective_id, split):
-    shape = x.shape if split else (NMP,) + x.shape
-    return pl.pallas_call(
-        functools.partial(mp_exchange_kernel, split),
-        out_shape=jax.ShapeDtypeStruct(shape, x.dtype),
-        in_specs=[VMEM],
-        out_specs=VMEM,
-        scratch_shapes=[
-            pltpu.SemaphoreType.DMA((NMP,)),
-            pltpu.SemaphoreType.DMA((NMP,)),
-            pltpu.SemaphoreType.DMA,
-        ],
-        compiler_params=pltpu.CompilerParams(
-            collective_id=collective_id, has_side_effects=True
-        ),
-    )(x)
-
-
-def spread_kernel(src, out, send_sem, recv_sem, own_sem):
-    psg = lax.axis_index("psg")
-    mp = lax.axis_index("mp")
-    x = psg // 8
-    mine = x == mp
-
-    def greet(k, c):
-        frm = lax.rem(psg + k, NPSG)
-
-        @pl.when(jnp.logical_or(k > 0, jnp.logical_not(mine)))
-        def _():
-            signal((frm, x))
-
-        return c
-
-    lax.fori_loop(0, NPSG, greet, 0)
-    first = lax.rem(psg, 8) * 4 + mp
-
-    def copy(k):
-        t = lax.rem(first + k, NPSG)
-        c, m = t // 4, lax.rem(t, 4)
-        return remote(src.at[c, m], out.at[psg], send_sem.at[k], recv_sem.at[psg], (mp * 8 + c, m))
-
-    @pl.when(mine)
-    def _():
-        own = pltpu.make_async_copy(src.at[lax.rem(psg, 8), mp], out.at[psg], own_sem)
-        own.start()
-        own.wait()
-        pl.semaphore_wait(pltpu.get_barrier_semaphore(), NPSG - 1)
-
-    @pl.when(jnp.logical_not(mine))
-    def _():
-        pl.semaphore_wait(pltpu.get_barrier_semaphore(), NPSG)
-        copy(0).start()
-
-    def start(k, c):
-        copy(k).start()
-        return c
-
-    lax.fori_loop(1, NPSG, start, 0)
-
-    def arrived(k, c):
-        frm = lax.rem(psg + k, NPSG)
-        remote(src.at[0, 0], out.at[frm], send_sem.at[0], recv_sem.at[frm], (frm, x)).wait_recv()
-        return c
-
-    def sent(k, c):
-        copy(k).wait_send()
-        return c
-
-    @pl.when(jnp.logical_not(mine))
-    def _():
-        arrived(0, 0)
-        copy(0).wait_send()
-
-    lax.fori_loop(1, NPSG, arrived, 0)
-    lax.fori_loop(1, NPSG, sent, 0)
-
-
-def spread(x, collective_id):
-    return pl.pallas_call(
-        spread_kernel,
-        out_shape=jax.ShapeDtypeStruct((NPSG,) + x.shape[2:], x.dtype),
-        in_specs=[VMEM],
-        out_specs=VMEM,
-        scratch_shapes=[
-            pltpu.SemaphoreType.DMA((NPSG,)),
-            pltpu.SemaphoreType.DMA((NPSG,)),
-            pltpu.SemaphoreType.DMA,
-        ],
-        compiler_params=pltpu.CompilerParams(
-            collective_id=collective_id, has_side_effects=True
-        ),
-    )(x)
-
-
-def lookup_kernel(ids, base, table, out, rows, sems):
+def lookup_kernel(ids, lengths, assignment, retrieval, table, out, mask_add, claims, extra, rows, sems):
     copies = []
     held = []
+    base = lax.axis_index("mp") * table.shape[0]
     for i in range(CLAIMS * POS):
-        local = ids[i] - base[0]
+        local = ids[i % POS, i // POS] - base
         inside = jnp.logical_and(local >= 0, local < table.shape[0])
         local = jnp.clip(local, 0, table.shape[0] - 1)
         start = pl.multiple_of((local // 16) * 16, 16)
@@ -260,6 +91,12 @@
             pltpu.make_async_copy(table.at[pl.ds(start, 16), :], rows.at[i], sems.at[i])
         )
         copies[-1].start()
+    slot = lax.broadcasted_iota(jnp.int32, (16, SEQ), 1)
+    for p in range(4):
+        add = jnp.where(slot < lengths[p], 0.0, MASKED)
+        mask_add[p] = add[:8]
+        extra[p] = add + retrieval[p]
+        claims[p] = jnp.zeros((16, SEQ), jnp.int32) + assignment[p]
     at = lax.broadcasted_iota(jnp.int32, (16, 128), 0)
     for i in range(CLAIMS * POS):
         copies[i].wait()
@@ -267,18 +104,24 @@
         out[pl.ds(i, 1), :] = jnp.sum(picked, axis=0, keepdims=True)
 
 
-def lookup(ids, base, table):
+def lookup(ids, lengths, assignment, retrieval, table):
     smem = pl.BlockSpec(memory_space=pltpu.SMEM)
+    f32 = jnp.float32
     return pl.pallas_call(
         lookup_kernel,
-        out_shape=jax.ShapeDtypeStruct((CLAIMS * POS, 128), jnp.float32),
-        in_specs=[smem, smem, ANY],
-        out_specs=VMEM,
+        out_shape=(
+            jax.ShapeDtypeStruct((CLAIMS * POS, 128), f32),
+            jax.ShapeDtypeStruct((4, 8, SEQ), f32),
+            jax.ShapeDtypeStruct((4, 16, SEQ), jnp.int32),
+            jax.ShapeDtypeStruct((4, 16, SEQ), f32),
+        ),
+        in_specs=[smem] * 4 + [ANY],
+        out_specs=(VMEM,) * 4,
         scratch_shapes=[
             pltpu.VMEM((CLAIMS * POS, 16, 128), jnp.bfloat16),
             pltpu.SemaphoreType.DMA((CLAIMS * POS,)),
         ],
-    )(ids, base, table)
+    )(ids, lengths, assignment, retrieval, table)
 
 
 def split3(values):
@@ -316,9 +159,11 @@
     dec_gain,
     cross_query,
     cross_keyval,
+    cross_output,
+    claims,
+    extra,
     enc_out,
-    u_out,
-    emb_out,
+    dec_out,
     g_ref,
     normed,
     acc,
@@ -332,6 +177,26 @@
     mp_buf,
     x_buf,
     yz_buf,
+    sc_src,
+    sc_in,
+    all_w,
+    all_st,
+    lhs,
+    y_src,
+    y_zin,
+    st_z,
+    y_one,
+    y_ysrc,
+    y_yin,
+    st_one,
+    st_yin,
+    y_two,
+    st_two,
+    y_in,
+    st_in,
+    x_buf2,
+    yz_buf2,
+    mp_buf2,
     send_sem,
     recv_sem,
     own_sem,
@@ -396,6 +261,13 @@
         def _():
             signal((frm, m))
 
+    for k in range(4):
+        frm = psg_of(lax.rem(x + k, 4), yl, z)
+        if k == 0:
+            pl.when(jnp.logical_not(mine))(functools.partial(signal, (frm, x)))
+        else:
+            signal((frm, x))
+
     def g(k, xs, zs, yls, cols=None):
         rows = ALL if yls is None else pl.ds(pl.multiple_of(yls * 128, 128), 128)
         c = ALL if cols is None else pl.ds(cols[0], cols[1])
@@ -440,7 +312,7 @@
             self.f_up.wait_recv()
             self.f_down.wait_recv()
 
-    pl.semaphore_wait(pltpu.get_barrier_semaphore(), jnp.where(mine, 18, 19))
+    pl.semaphore_wait(pltpu.get_barrier_semaphore(), jnp.where(mine, 21, 23))
 
     yd = send(0, w_ref.at[0], g(0, x, z, yl), y_dev)
     ye = send(1, w_ref.at[1], g(1, x, z, yl), y_dev)
@@ -463,7 +335,6 @@
     for copy in mps:
         copy.wait_recv()
     emb = mp_buf[0] + mp_buf[1] + mp_buf[2] + mp_buf[3]
-    emb_out[...] = emb
     terms = dot3(emb * dec_gain[...], cross_query[...])
     squares = jnp.sum(emb * emb, axis=1, keepdims=True)
     x_buf[x, :, pl.ds(0, 512)] = terms
@@ -654,7 +525,7 @@
                 s = lax.dot_general(
                     qt, k2, (((1,), (1,)), ((), ())), preferred_element_type=f32
                 )
-                s = s + bias[2 * j + t] + mask_add[pl.ds(p, 1), :]
+                s = s + bias[2 * j + t] + mask_add[p, pl.ds(0, 1), :]
                 wts = jnp.exp(s - jnp.max(s, axis=1, keepdims=True))
                 scale = 1.0 / jnp.sum(wts, axis=1, keepdims=True)
                 outs.append(
@@ -716,11 +587,7 @@
     ef_down.wait_recv()
     hand_over(2)
     hand_over(3)
-    u_copy = pltpu.make_async_copy(e_ref.at[:, pl.ds(512, 128), :], u_out, own_sem.at[5])
-    u_copy.start()
-    for p in range(4):
-        cores[p].wait_recv()
-        lasts[p].wait_recv()
+    def out_project(p):
         rows = pl.ds(p * SEQ, SEQ)
 
         def out_cols(i, c):
@@ -736,29 +603,237 @@
 
         lax.fori_loop(0, 2, out_cols, 0)
 
-    u_copy.wait()
+    def cross_scores(p):
+        enc = enc_out[pl.ds(p * SEQ, SEQ), :]
+        wide_enc = enc.astype(f32)
+        squares = jnp.sum(wide_enc * wide_enc, axis=1, keepdims=True)
+        squares = jnp.broadcast_to(squares, (SEQ, 128)).T[:8]
+        for m in range(NMP):
+            both = lax.dot_general(
+                e_ref[m, pl.ds(512, 128), :], enc, (((1,), (1,)), ((), ())),
+                preferred_element_type=f32,
+            )
+            both = both[:64] + both[64:]
+            picked = jnp.zeros((16, SEQ), f32)
+            for c in range(CLAIMS):
+                picked = jnp.where(claims[p] == c, both[c * 16 : (c + 1) * 16], picked)
+            sc_src[m, p, pl.ds(0, 16), :] = picked
+            sc_src[m, p, pl.ds(16, 8), :] = squares
+        out = []
+        for k in range(1, 4):
+            to = lax.rem(mp + k, NMP)
+            out.append(
+                send(84 + p * 3 + k - 1, sc_src.at[to, p], sc_in.at[mp, p], mp_dev(k))
+            )
+        sc_in[mp, p] = sc_src[mp, p]
+        return out
+
+    scs = []
+    for p in range(4):
+        cores[p].wait_recv()
+        lasts[p].wait_recv()
+        out_project(p)
+        scs.append(cross_scores(p))
+
+    crosses, inverses, maxima = [], [], []
+    for p in range(4):
+        for copy in scs[p]:
+            copy.wait_recv()
+        raw = sc_in[0, p] + sc_in[1, p] + sc_in[2, p] + sc_in[3, p]
+        inverse = lax.rsqrt(raw[16:17] / D + EPSILON)
+        cross = raw[:16] * inverse + extra[p]
+        crosses.append(cross)
+        inverses.append(inverse)
+        maxima.append(jnp.broadcast_to(jnp.max(cross, axis=1, keepdims=True), (16, SEQ)))
+    claim_max = []
+    for c in range(CLAIMS):
+        top = jnp.full((16, SEQ), MASKED, f32)
+        for p in range(4):
+            top = jnp.maximum(top, jnp.where(claims[p] == c, maxima[p], MASKED))
+        claim_max.append(top)
+    sums = []
+    for p in range(4):
+        chosen = claim_max[0]
+        for c in range(1, CLAIMS):
+            chosen = jnp.where(claims[p] == c, claim_max[c], chosen)
+        wts = jnp.exp(crosses[p] - chosen)
+        sums.append(jnp.broadcast_to(jnp.sum(wts, axis=1, keepdims=True), (16, SEQ)))
+        all_w[mp, p] = (wts * inverses[p]).astype(bf16)
+    totals = []
+    for c in range(CLAIMS):
+        total = jnp.zeros((16, SEQ), f32)
+        for p in range(4):
+            total = total + jnp.where(claims[p] == c, sums[p], 0.0)
+        totals.append(total)
+    first_row = lax.broadcasted_iota(jnp.int32, (8, 128), 0) == 0
+
+    def lanes_of(parts, fill):
+        column = jnp.concatenate([part[:, :128] for part in parts], axis=0)
+        column = jnp.concatenate([column, jnp.full((64, 128), fill, f32)], axis=0)
+        return column.T[:8]
+
+    all_st[mp] = jnp.where(first_row, lanes_of(claim_max, MASKED), lanes_of(totals, 0.0))
+    ws = [send(96 + k, all_w.at[mp], all_w.at[mp], mp_dev(k)) for k in range(3 + 1) if k]
+    sts = [send(99 + k, all_st.at[mp], all_st.at[mp], mp_dev(k)) for k in range(3 + 1) if k]
+    for copy in ws + sts:
+        copy.wait_recv()
+
+    for p in range(4):
+        for m in range(NMP):
+            w_mp = all_w[m, p].astype(f32)
+            for c in range(CLAIMS):
+                lhs[p, pl.ds(m * 64 + c * 16, 16), :] = jnp.where(
+                    claims[p] == c, w_mp, 0.0
+                ).astype(bf16)
+    for i in range(2):
+        total = None
+        for p in range(4):
+            term = jnp.dot(
+                lhs[p], enc_out[pl.ds(p * SEQ, SEQ), pl.ds(i * 512, 512)],
+                preferred_element_type=f32,
+            )
+            total = term if total is None else total + term
+        for zt in range(4):
+            y_src[zt, i] = total[:, zt * 128 : (zt + 1) * 128].astype(bf16)
+    y_copies, st_copies = [], []
+    for k in range(1, 4):
+        tz = lax.rem(z + k, 4)
+        y_copies.append(send(103 + k, y_src.at[tz], y_zin.at[z], dev("z", k)))
+        st_copies.append(send(106 + k, all_st, st_z.at[z], dev("z", k)))
+    y_zin[z] = y_src[z]
+    st_z[z] = all_st[...]
+
+    def merge(stats, rows):
+        top = stats[0][0:1]
+        for st in stats[1:]:
+            top = jnp.maximum(top, st[0:1])
+        total = jnp.zeros((1, 128), f32)
+        results = [jnp.zeros((64, 128), f32) for _ in rows[0]]
+        for st, these in zip(stats, rows):
+            scale = jnp.exp(st[0:1] - top)
+            total = total + scale * st[1:2]
+            column = jnp.broadcast_to(scale, (128, 128)).T[:64]
+            results = [r + column * t.astype(f32) for r, t in zip(results, these)]
+        both = jnp.where(
+            first_row, jnp.broadcast_to(top, (8, 128)), jnp.broadcast_to(total, (8, 128))
+        )
+        return both, results
+
+    for copy in y_copies + st_copies:
+        copy.wait_recv()
+    for m in range(NMP):
+        part = pl.ds(m * 64, 64)
+        both, results = merge(
+            [st_z[j, m] for j in range(4)],
+            [[y_zin[j, i, part, :] for i in range(2)] for j in range(4)],
+        )
+        st_one[m] = both
+        for i in range(2):
+            y_one[i, m] = results[i]
+    y_ysrc[...] = y_one[1 - yl].astype(bf16)
+    yc = send(110, y_ysrc, y_yin, y_dev)
+    ystc = send(111, st_one, st_yin, y_dev)
+    yc.wait_recv()
+    ystc.wait_recv()
+    for m in range(NMP):
+        both, results = merge([st_one[m], st_yin[m]], [[y_one[yl, m]], [y_yin[m]]])
+        st_two[m] = both
+        y_two[m] = results[0]
+
+    def to_owner(k):
+        m = lax.rem(mp + k, NMP)
+        target = (psg_of(mp, yl, z), m)
+        return (
+            remote(y_two.at[m], y_in.at[x], send_sem.at[112 + k], recv_sem.at[112 + x], target),
+            remote(st_two.at[m], st_in.at[x], send_sem.at[116 + k], recv_sem.at[116 + x], target),
+        )
+
+    def from_source(k):
+        frm = lax.rem(x + k, 4)
+        target = (psg_of(frm, yl, z), x)
+        return (
+            remote(y_two.at[0], y_in.at[frm], send_sem.at[112], recv_sem.at[112 + frm], target),
+            remote(st_two.at[0], st_in.at[frm], send_sem.at[116], recv_sem.at[116 + frm], target),
+        )
+
+    @pl.when(mine)
+    def _():
+        y_in[x] = y_two[mp]
+        st_in[x] = st_two[mp]
+
+    @pl.when(jnp.logical_not(mine))
+    def _():
+        for copy in to_owner(0):
+            copy.start()
+
+    for k in range(1, 4):
+        for copy in to_owner(k):
+            copy.start()
+
+    @pl.when(jnp.logical_not(mine))
+    def _():
+        for copy in from_source(0):
+            copy.wait_recv()
+
+    for k in range(1, 4):
+        for copy in from_source(k):
+            copy.wait_recv()
+    both, results = merge([st_in[j] for j in range(4)], [[y_in[j]] for j in range(4)])
+    total = jnp.broadcast_to(both[1:2], (128, 128)).T[:64]
+    mean_rows = results[0] / total
+    mean_rows = mean_rows * final_gain[:, pl.ds(pl.multiple_of(psg * 128, 128), 128)]
+
+    products = dot3(mean_rows, cross_keyval[1])
+    products = jnp.where(head_of_row == head_of_lane, products, 0.0)
+    x_buf2[x] = jnp.sum(products.reshape(8, 8, 512), axis=1)
+    xs = [send(120 + k, x_buf2.at[x], x_buf2.at[x], dev("x", k)) for k in range(1, 4)]
+    for copy in xs:
+        copy.wait_recv()
+    yz_buf2[yz] = x_buf2[0] + x_buf2[1] + x_buf2[2] + x_buf2[3]
+    yzs = [send(124 + k, yz_buf2.at[yz], yz_buf2.at[yz], yz_dev(k)) for k in range(1, 8)]
+    for copy in yzs:
+        copy.wait_recv()
+    cross_attn = yz_buf2[0]
+    for k in range(1, 8):
+        cross_attn = cross_attn + yz_buf2[k]
+    mp_buf2[mp] = dot3(cross_attn, cross_output[...])
+    lasts = [send(132 + k, mp_buf2.at[mp], mp_buf2.at[mp], mp_dev(k)) for k in range(1, 4)]
+    for copy in lasts:
+        copy.wait_recv()
+    final = (mp_buf2[0] + mp_buf2[1] + mp_buf2[2] + mp_buf2[3]) + (
+        mp_buf[0] + mp_buf[1] + mp_buf[2] + mp_buf[3]
+    )
+    share = final[:, :32]
+    for m in range(1, NMP):
+        share = jnp.where(mp == m, final[:, m * 32 : (m + 1) * 32], share)
+    dec_out[...] = share.astype(bf16)
+
     for copy in sent:
         copy.wait_send()
     for k in range(1, 4):
         block_copy(k).wait_send()
+        for copy in to_owner(k):
+            copy.wait_send()
 
     @pl.when(jnp.logical_not(mine))
     def _():
         block_copy(0).wait_send()
+        for copy in to_owner(0):
+            copy.wait_send()
 
 
 def encoder(args):
     tok_rows = args[0].shape[0]
     bf16 = jnp.bfloat16
+    f32 = jnp.float32
     return pl.pallas_call(
         encoder_kernel,
         out_shape=(
             jax.ShapeDtypeStruct((tok_rows, 1024), bf16),
-            jax.ShapeDtypeStruct((NMP, 128, 1024), bf16),
-            jax.ShapeDtypeStruct((CLAIMS * POS, 128), jnp.float32),
+            jax.ShapeDtypeStruct((CLAIMS * POS, 32), bf16),
         ),
-        in_specs=[ANY, VMEM, ANY, VMEM, VMEM, VMEM, ANY] + [VMEM] * 5,
-        out_specs=(VMEM, ANY, VMEM),
+        in_specs=[ANY, VMEM, ANY, VMEM, VMEM, VMEM, ANY] + [VMEM] * 8,
+        out_specs=(VMEM, VMEM),
         scratch_shapes=[
             pltpu.VMEM((3, 4, 4, 256, 512), bf16),
             pltpu.VMEM((tok_rows, D), bf16),
@@ -772,21 +847,35 @@
             pltpu.VMEM((640, 128), bf16),
             pltpu.VMEM((NMP, 8, 128), jnp.float32),
             pltpu.VMEM((4, 8, 640), jnp.float32),
-            pltpu.VMEM((8, 8, 640), jnp.float32),
-            pltpu.SemaphoreType.DMA((84,)),
-            pltpu.SemaphoreType.DMA((84,)),
-            pltpu.SemaphoreType.DMA((6,)),
+            pltpu.VMEM((8, 8, 640), f32),
+            pltpu.VMEM((NMP, 4, 24, SEQ), f32),
+            pltpu.VMEM((NMP, 4, 24, SEQ), f32),
+            pltpu.VMEM((NMP, 4, 16, SEQ), bf16),
+            pltpu.VMEM((NMP, 8, 128), f32),
+            pltpu.VMEM((4, 256, SEQ), bf16),
+            pltpu.VMEM((4, 2, 256, 128), bf16),
+            pltpu.VMEM((4, 2, 256, 128), bf16),
+            pltpu.VMEM((4, NMP, 8, 128), f32),
+            pltpu.VMEM((2, NMP, 64, 128), f32),
+            pltpu.VMEM((NMP, 64, 128), bf16),
+            pltpu.VMEM((NMP, 64, 128), bf16),
+            pltpu.VMEM((NMP, 8, 128), f32),
+            pltpu.VMEM((NMP, 8, 128), f32),
+            pltpu.VMEM((NMP, 64, 128), f32),
+            pltpu.VMEM((NMP, 8, 128), f32),
+            pltpu.VMEM((4, 64, 128), f32),
+            pltpu.VMEM((4, 8, 128), f32),
+            pltpu.VMEM((4, 8, 512), f32),
+            pltpu.VMEM((8, 8, 512), f32),
+            pltpu.VMEM((NMP, 8, 128), f32),
+            pltpu.SemaphoreType.DMA((136,)),
+            pltpu.SemaphoreType.DMA((136,)),
+            pltpu.SemaphoreType.DMA((5,)),
         ],
         compiler_params=pltpu.CompilerParams(
             collective_id=1, has_side_effects=True, vmem_limit_bytes=58 << 20
         ),
     )(*args)
-
-
-def high_low(values):
-    high = values.astype(jnp.bfloat16)
-    low = (values - high.astype(jnp.float32)).astype(jnp.bfloat16)
-    return high, low
 
 
 def shards(
@@ -806,21 +895,12 @@
     cross_keyval,
     cross_output,
 ):
-    f32 = jnp.float32
-    psg = lax.axis_index("psg")
-    mp = lax.axis_index("mp")
-    tok_rows = tokens.shape[0]
-    passages_here = lengths.shape[0]
-    heads_here = enc_qkv.shape[2] // HEAD_DIM
-    query_rows = CLAIMS * POS
-    positions = jnp.arange(SEQ)
-
-    vocab_here = embedding.shape[0]
-    found = lookup(dec_tokens.reshape(-1), (mp * vocab_here).reshape(1), embedding)
+    found, mask_add, claims, extra = lookup(
+        dec_tokens.T, lengths, assignment, retrieval, embedding
+    )
     onehot = bucket_onehot(SEQ, BUCKETS, MAXDIST)
     onehot = np.concatenate([onehot[:, 255:], np.zeros((BUCKETS, 1)), onehot[:, :255]], axis=1)
-    mask_add = jnp.where(positions[None, :] < lengths[:, None], 0.0, MASKED)
-    encoded, u_all, embedded = encoder(
+    encoded, decoded = encoder(
         (
             tokens,
             enc_gain.reshape(1, D),
@@ -834,80 +914,12 @@
             dec_gain.reshape(1, 128),
             cross_query,
             cross_keyval,
+            cross_output,
+            claims,
+            extra,
         )
     )
-    width = encoded.shape[1]
-    gain_here = lax.dynamic_slice_in_dim(final_gain, psg * 128, 128, 0)
-    encoded_f = encoded.astype(f32)
-    squares = jnp.sum(encoded_f * encoded_f, axis=1).reshape(passages_here, SEQ)
-
-    rows_u = u_all.reshape(NMP, 2, CLAIMS, POS * heads_here, width)
-    claim_u = jnp.stack(
-        [lax.dynamic_index_in_dim(rows_u, assignment[i], 2, False) for i in range(passages_here)],
-        axis=2,
-    )
-    per_psg = encoded.reshape(passages_here, SEQ, width)
-    partial = jnp.einsum("mapnd,pkd->mapnk", claim_u, per_psg, preferred_element_type=f32)
-    partial = (partial[:, 0] + partial[:, 1]).reshape(NMP, passages_here * POS * heads_here, SEQ)
-    extra = jnp.broadcast_to(
-        jnp.concatenate([squares, jnp.zeros_like(squares)], axis=0)[None],
-        (NMP, 2 * passages_here, SEQ),
-    )
-    raw = jnp.sum(mp_exchange(jnp.concatenate([partial, extra], axis=1), 5, True), axis=0)
-    n_rows = passages_here * POS * heads_here
-    inverse = lax.rsqrt(raw[n_rows : n_rows + passages_here] / D + EPSILON)
-    cross = raw[:n_rows].reshape(passages_here, POS * heads_here, SEQ)
-    cross = cross * inverse[:, None, :] + retrieval[:, None, None]
-    usable = (positions[None, :] < lengths[:, None])[:, None, :]
-    masked = jnp.where(usable, cross, MASKED)
-    onehot = assignment[None, :] == jnp.arange(CLAIMS)[:, None]
-    psg_max = jnp.max(masked, axis=-1)
-    local_max = jnp.max(jnp.where(onehot[:, :, None], psg_max[None], MASKED), axis=1)
-    chosen_max = jnp.max(jnp.where(onehot[:, :, None], local_max[:, None], MASKED), axis=0)
-    weights_c = jnp.where(
-        usable, jnp.exp(masked - chosen_max[:, :, None]), 0.0
-    )
-    local_total = jnp.sum(
-        jnp.where(onehot[:, :, None], jnp.sum(weights_c, axis=-1)[None], 0.0), axis=1
-    )
-    stats = jnp.stack([local_max.reshape(-1), local_total.reshape(-1)])
-    stats = jnp.pad(stats, ((0, 6), (0, SEQ - stats.shape[1])))
-    sent = jnp.concatenate(
-        [(weights_c * inverse[:, None, :]).reshape(n_rows, SEQ), stats], axis=0
-    )
-    all_w = mp_exchange(sent, 6, False)
-    spread_w = jnp.where(
-        onehot[None, :, :, None, None],
-        all_w[:, :n_rows].reshape(NMP, 1, passages_here, POS * heads_here, SEQ),
-        0.0,
-    )
-    w_high, w_low = high_low(spread_w)
-    weighted = jnp.einsum(
-        "mcpnk,pkd->mcnd", w_high, per_psg, preferred_element_type=f32
-    ) + jnp.einsum("mcpnk,pkd->mcnd", w_low, per_psg, preferred_element_type=f32)
-    weighted = weighted.reshape(NMP, query_rows * heads_here, 8, 128).transpose(2, 0, 1, 3)
-    both = jnp.concatenate([all_w[:, n_rows, :64], all_w[:, n_rows + 1, :64]], axis=1)
-    both = jnp.broadcast_to(
-        jnp.pad(both[:, None, :], ((0, 0), (0, 7), (0, 0)))[None], (8, NMP, 8, 128)
-    )
-    got = spread(jnp.concatenate([weighted, both], axis=2), 7)
-    each_max = got[:, 64, :64]
-    each_total = got[:, 64, 64:]
-    joint_max = jnp.max(each_max, axis=0)
-    scale = jnp.exp(each_max - joint_max[None])
-    total = jnp.sum(scale * each_total, axis=0)
-    mean_rows = jnp.sum(got[:, :64] * scale[:, :, None], axis=0) / total[:, None] * gain_here
-    attn_part = jnp.einsum(
-        "rhc,chd->rhd",
-        mean_rows.reshape(query_rows, heads_here, 128),
-        cross_keyval[1].astype(f32).reshape(128, heads_here, HEAD_DIM),
-        precision=HIGHEST,
-    ).reshape(query_rows, 512)
-    cross_attn = jnp.sum(psg_gather(attn_part, 8), axis=0)
-    out_part = jnp.dot(cross_attn, cross_output.astype(f32), precision=HIGHEST)
-    out_sum = jnp.sum(mp_exchange(out_part, 9, False), axis=0) + embedded
-    decoded = lax.dynamic_slice_in_dim(out_sum, mp * 32, 32, 1)
-    return (encoded, decoded.astype(jnp.bfloat16).reshape(CLAIMS, POS, 32))
+    return (encoded, decoded.reshape(CLAIMS, POS, 32))
 
 
 def solution(mesh):

time: 286 us -> 230 us (0.80)
  Pallas kernels: 252 us -> 226 us
  other arithmetic: 9.01 us -> 0 us
  local copies, waits for them, and re-layouts: 12.3 us -> 3.66 us
  between operations: 8.56 us -> 0.66 us
  matrix products: 3.39 us -> 0 us
    pallas_call x6 -> x1, Pallas kernels: 80.8 us -> 2.34 us  [lookup(): pl.pallas_call(lookup_kernel, out_shape=(jax.ShapeDtypeStruct((CLAIMS * P...]
    pallas_call x1, Pallas kernels: 171 us -> 223 us  [encoder(): pl.pallas_call(encoder_kernel, out_shape=(jax.ShapeDtypeStruct((tok_rows,...]
    reduce_sum x7 -> x0, other arithmetic: 4.98 us -> none  [the longest x1 1.57 us: shards(): jnp.sum(got[:, :64] * scale[:, :, None], axis=0) / total[:, None]]
    slice x7 -> x0, local copies, waits for them, and re-layouts: 4.44 us -> none  [the longest x1 1.48 us: shards(): assignment[i]]
    dot_general x5 -> x0, matrix products: 3.39 us -> none  [the longest x1 0.83 us: shards(): jnp.einsum('mapnd,pkd->mapnk', claim_u, per_psg, preferred_element_type=f32)]
where the time goes in v3:
time: 230 us
  Pallas kernels  226 us (98%)
  local copies, waits for them, and re-layouts  3.66 us (2%)
    pallas_call x1, Pallas kernels, encoder(): pl.pallas_call(encoder_kernel, out_shape=(jax.ShapeDtypeStruct((tok_rows,...  223 us

profile of v3, /device:TPU:1, one launch (start us, length us, event | category | flops | bytes accessed | tf_op | source)
XLA Modules:
  0.0 229.9 jit_solution(7000809742984474403)
XLA Ops:
  0.6 2.3 %shard_map.167 = (f32[8,128]{1,0:T(8,128)}, f32[4,8,256]{2,1,0:T(8,128)}, s32[4,16,256]{2,1,0:T(8,128)}, f32[4,16,256]{2,1,0:T(8,128)}) custom-call(s32[2,4]{1,0:T(2,128)} %bitcast.8, s32[4]{0:T(128)} %lengths.1, s32[4]{0:T(128)} %assignment.1, f32[4]{0:T(128)} %retrieval.1, bf16[8032,128]{1,0:T(8,128)(2,1)} %table.1), custom_call_target="tpu_custom_call" | custom-call | tf_op jit(solution)/shard_map/pallas_call | solution.py:110
  3.0 223.2 %shard_map.168 = (bf16[1024,1024]{1,0:T(8,128)(2,1)}, bf16[8,32]{1,0:T(8,128)(2,1)}) custom-call(bf16[1024,4096]{1,0:T(8,128)(2,1)} %tokens.1, f32[1,4096]{1,0:T(1,128)} %bitcast.5, bf16[3,128,512]{2,1,0:T(8,128)(2,1)} %w_ref.1, f32[8,32]{1,0:T(8,128)} %bias_in.1, bf16[32,512]{1,0:T(8,128)(2,1)} %constant.2.clone.onehot, ...), custom_call_target="tpu_custom_call" | custom-call | tf_op jit(solution)/shard_map/pallas_call | solution.py:829
  226.2 0.0 copy-start
  226.2 3.1 %copy.20 = bf16[1024,1024]{1,0:T(8,128)(2,1)} copy(bf16[1024,1024]{1,0:T(8,128)(2,1)} %get-tuple-element.16) | data formatting | bytes 4194304
  229.3 0.0 copy-done
  229.3 0.6 copy.21
Async XLA Ops:
  226.2 3.1 %copy-start = (bf16[8,32]{1,0:T(8,128)(2,1)S(1)}, bf16[8,32]{1,0:T(8,128)(2,1)}, u32[]{:S(2)}) copy-start(bf16[8,32]{1,0:T(8,128)(2,1)} %get-tuple-element.13) | copy-start | bytes 1540

commit v4 on v3

--- a/solution.py
+++ b/solution.py
@@ -169,6 +169,7 @@
     acc,
     qkv,
     e_ref,
+    u_ref,
     att,
     transit,
     bias,
@@ -229,9 +230,7 @@
     same_half = (x // 2) == yh
     yl_to = jnp.where(same_half, yl, 1 - yl)
 
-    def block_to(k):
-        return (psg_of(lax.rem(x + k, 4), yl_to, z), x)
-
+    block_to = (psg_of(x, yl_to, z), x)
     mine = x == mp
 
     load_tokens = pltpu.make_async_copy(tokens, normed, own_sem.at[0])
@@ -244,9 +243,6 @@
         tokens.at[:, pl.ds(pl.multiple_of(mp * 1024, 128), 1024)], tok_here, own_sem.at[2]
     )
     load_here.start()
-    load_block = pltpu.make_async_copy(enc_output, block.at[pl.ds(0, 512)], own_sem.at[3])
-    load_block.start()
-
     for k in range(1, 4):
         signal(dev("x", k))
         signal(mp_dev(k))
@@ -254,12 +250,12 @@
         signal(yz_dev(k))
     signal(y_step(1))
     signal(y_step(3))
-    for m in range(NMP):
-        frm = psg_of(mp, jnp.where((m // 2) == yh, yl, 1 - yl), z)
-
-        @pl.when(jnp.logical_not(jnp.logical_and(mine, m == mp)))
-        def _():
-            signal((frm, m))
+
+    @pl.when(mine)
+    def _():
+        for k in range(1, 4):
+            m = lax.rem(mp + k, NMP)
+            signal((psg_of(x, jnp.where((m // 2) == yh, yl, 1 - yl), z), m))
 
     for k in range(4):
         frm = psg_of(lax.rem(x + k, 4), yl, z)
@@ -298,21 +294,133 @@
             self.up = send(t, src, piece(self.at), dev(axis, 1))
             self.down = send(t + 1, src, piece(self.at), dev(axis, 3))
 
-        def forward(self):
+        def forward(self, then=None):
             below = lax.rem(self.at + 3, 4)
             above = lax.rem(self.at + 1, 4)
             self.up.wait_recv()
             up = self.piece(below, 0)
             self.f_up = send(self.t + 2, up, up, dev(self.axis, 1))
+            if then is not None:
+                then(1, below)
             self.down.wait_recv()
             down = self.piece(above, 1)
             self.f_down = send(self.t + 3, down, down, dev(self.axis, 3))
-
-        def end(self):
+            if then is not None:
+                then(2, above)
+
+        def end(self, then=None):
             self.f_up.wait_recv()
             self.f_down.wait_recv()
-
-    pl.semaphore_wait(pltpu.get_barrier_semaphore(), jnp.where(mine, 21, 23))
+            if then is not None:
+                then(3, lax.rem(self.at + 2, 4))
+
+    go_step = jnp.where(core == 1, 1, 3)
+    go_on = lax.rem(mp + go_step, 4) == x
+    near = pl.ds(yh * 2, 2)
+    far_half = pl.ds(2 - yh * 2, 2)
+
+    class Blocks:
+        def __init__(self, t, src, ref, own_t):
+            self.t, self.ref, self.src = t, ref, src
+            first = self.at(mp, yl, z)
+            self.block = remote(src, first, send_sem.at[t], recv_sem.at[t + 1 + mp], block_to)
+            self.keep = pltpu.make_async_copy(src, first, own_sem.at[own_t])
+            n, f = self.at(near, yl, z), self.at(far_half, 1 - yl, z)
+            self.ys = [
+                remote(n, n, send_sem.at[t + 5], recv_sem.at[t + 5], y_dev),
+                remote(f, f, send_sem.at[t + 6], recv_sem.at[t + 6], y_dev),
+            ]
+
+        def at(self, ms, yls, zs):
+            col = pl.multiple_of((yls * 4 + zs) * 128, 128)
+            return self.ref.at[ms, :, pl.ds(col, 128)]
+
+        def x_copy(self, c, step, t):
+            part = self.at(ALL, c, z)
+            return remote(
+                part, part, send_sem.at[self.t + t], recv_sem.at[self.t + 13 + c], dev("x", step)
+            )
+
+        def start(self):
+            pl.when(mine)(self.keep.start)
+            pl.when(jnp.logical_not(mine))(self.block.start)
+
+        def across(self):
+            @pl.when(mine)
+            def _():
+                for k in range(1, 4):
+                    m = lax.rem(mp + k, NMP)
+                    remote(
+                        self.src,
+                        self.at(m, yl, z),
+                        send_sem.at[self.t],
+                        recv_sem.at[self.t + 1 + m],
+                        y_dev,
+                    ).wait_recv()
+                self.keep.wait()
+                for copy in self.ys:
+                    copy.start()
+
+        def along(self):
+            @pl.when(mine)
+            def _():
+                for copy in self.ys:
+                    copy.wait_recv()
+                for c in range(2):
+                    self.x_copy(c, 1, 7 + c).start()
+                    self.x_copy(c, 3, 9 + c).start()
+
+        def forward(self):
+            @pl.when(go_on)
+            def _():
+                for c in range(2):
+                    self.x_copy(c, 1, 7 + c).wait_recv()
+                    self.x_copy(c, go_step, 11 + c).start()
+
+        def arrive(self):
+            @pl.when(jnp.logical_not(jnp.logical_or(mine, go_on)))
+            def _():
+                for c in range(2):
+                    self.x_copy(c, 1, 7 + c).wait_recv()
+
+        def ring(self):
+            t = self.t
+            parts = [self.at(ALL, i, z) for i in range(2)]
+            self.up = [send(t + 15 + i, parts[i], parts[i], dev("z", 1)) for i in range(2)]
+            self.down = [send(t + 17 + i, parts[i], parts[i], dev("z", 3)) for i in (1, 0)]
+
+        def ring_forward(self):
+            self.up[0].wait_recv()
+            part = self.at(ALL, 0, lax.rem(z + 3, 4))
+            self.f_up = send(self.t + 19, part, part, dev("z", 1))
+            self.down[0].wait_recv()
+            part = self.at(ALL, 1, lax.rem(z + 1, 4))
+            self.f_down = send(self.t + 20, part, part, dev("z", 3))
+
+        def ring_end(self):
+            for copy in (self.up[1], self.down[1], self.f_up, self.f_down):
+                copy.wait_recv()
+
+        def finish(self):
+            @pl.when(mine)
+            def _():
+                for copy in self.ys:
+                    copy.wait_send()
+                for c in range(2):
+                    self.x_copy(c, 1, 7 + c).wait_send()
+                    self.x_copy(c, 3, 9 + c).wait_send()
+
+            pl.when(jnp.logical_not(mine))(self.block.wait_send)
+
+            @pl.when(go_on)
+            def _():
+                for c in range(2):
+                    self.x_copy(c, go_step, 11 + c).wait_send()
+
+    e_blocks = Blocks(188, enc_output, e_ref, 3)
+    u_blocks = Blocks(209, block, u_ref, 4)
+
+    pl.semaphore_wait(pltpu.get_barrier_semaphore(), jnp.where(mine, 18, 20))
 
     yd = send(0, w_ref.at[0], g(0, x, z, yl), y_dev)
     ye = send(1, w_ref.at[1], g(1, x, z, yl), y_dev)
@@ -324,13 +432,40 @@
     )
     mp_buf[mp] = found[...]
     mps = [send(52 + k, found, mp_buf.at[mp], mp_dev(k)) for k in range(1, 4)]
+    e_blocks.start()
     own.wait()
+
+    d3, e3, yas, ybs = [None] * 4, [None] * 4, [None] * 4, [None] * 4
+
+    def start_d3(i, u):
+        d3[i] = Ring(140 + 4 * i, "z", lambda v, c=None: g(0, u, v, None, wide(c)))
+
+    def start_e3(i, u):
+        e3[i] = Ring(156 + 4 * i, "x", lambda v, c=None: g(1, v, u, None, wide(c)))
+
+    def start_ya(i, u):
+        plane = g(2, ALL, u, yl, low_cols(None))
+        yas[i] = send(172 + i, plane, plane, y_dev)
+
+    def start_yb(i, u):
+        plane = g(2, u, ALL, yl, high_cols(None))
+        ybs[i] = send(176 + i, plane, plane, y_dev)
+
+    a1.forward()
+    b1.forward()
     yd.wait_recv()
     d2 = Ring(20, "x", lambda v, c=None: g(0, v, z, None, wide(c)))
     ye.wait_recv()
     e2 = Ring(24, "z", lambda v, c=None: g(1, x, v, None, wide(c)))
-    a1.forward()
-    b1.forward()
+    a1.end()
+    a2 = Ring(12, "z", lambda v, c=None: g(2, ALL, v, yl, low_cols(c)))
+    start_ya(0, z)
+    b1.end()
+    b2 = Ring(16, "x", lambda v, c=None: g(2, v, ALL, yl, high_cols(c)))
+    start_yb(0, x)
+    start_d3(0, x)
+    start_e3(0, z)
+    e_blocks.across()
 
     for copy in mps:
         copy.wait_recv()
@@ -341,10 +476,9 @@
     x_buf[x, :, pl.ds(512, 128)] = jnp.broadcast_to(squares, (8, 128))
     xs = [send(56 + k, x_buf.at[x], x_buf.at[x], dev("x", k)) for k in range(1, 4)]
 
-    a1.end()
-    a2 = Ring(12, "z", lambda v, c=None: g(2, ALL, v, yl, low_cols(c)))
-    b1.end()
-    b2 = Ring(16, "x", lambda v, c=None: g(2, v, ALL, yl, high_cols(c)))
+    e_blocks.along()
+    d2.forward(start_d3)
+    e2.forward(start_e3)
 
     load_tokens.wait()
 
@@ -362,24 +496,27 @@
 
         lax.fori_loop(first, first + count, body, 0)
 
-    norm_rows(0, 24)
-
+    a2.forward(start_ya)
+    b2.forward(start_yb)
+    d2.end(start_d3)
+    e2.end(start_e3)
+    norm_rows(0, 16)
+    d3[0].forward()
+    e3[0].forward()
+    a2.end(start_ya)
+    b2.end(start_yb)
     for copy in xs:
         copy.wait_recv()
     yz = yl * 4 + z
     yz_buf[yz] = x_buf[0] + x_buf[1] + x_buf[2] + x_buf[3]
     yzs = [send(60 + k, yz_buf.at[yz], yz_buf.at[yz], yz_dev(k)) for k in range(1, 8)]
-
-    d2.forward()
-    e2.forward()
-    norm_rows(24, 20)
-    d2.end()
-    d3 = Ring(28, "z", lambda v, c=None: g(0, ALL, v, None, wide(c)))
-    e2.end()
-    e3 = Ring(32, "x", lambda v, c=None: g(1, v, ALL, None, wide(c)))
-    a2.forward()
-    b2.forward()
-    norm_rows(44, 20)
+    norm_rows(16, 16)
+    d3[1].forward()
+    e3[1].forward()
+    e_blocks.forward()
+    norm_rows(32, 16)
+    d3[2].forward()
+    e3[2].forward()
 
     for copy in yzs:
         copy.wait_recv()
@@ -394,57 +531,21 @@
     folded = dot3(spread_q, cross_keyval[0], 1)
     folded = folded * final_gain[:, pl.ds(pl.multiple_of(psg * 128, 128), 128)]
     high = folded.astype(bf16)
-    load_block.wait()
-    block[pl.ds(512, 64), :] = high
-    block[pl.ds(576, 64), :] = (folded - high.astype(f32)).astype(bf16)
-
-    def e(ms, yls, zs):
-        col = pl.multiple_of((yls * 4 + zs) * 128, 128)
-        return e_ref.at[ms, :, pl.ds(col, 128)]
-
-    def block_copy(k):
-        return remote(block, e(mp, yl, z), send_sem.at[36 + k], recv_sem.at[40 + mp], block_to(k))
-
-    keep = pltpu.make_async_copy(block, e(mp, yl, z), own_sem.at[4])
-
-    @pl.when(mine)
-    def _():
-        keep.start()
-
-    @pl.when(jnp.logical_not(mine))
-    def _():
-        block_copy(0).start()
-
-    for k in range(1, 4):
-        block_copy(k).start()
-
-    a2.end()
-    low = g(2, ALL, ALL, yl, low_cols(None))
-    ya = send(2, low, low, y_dev)
-    b2.end()
-    hi = g(2, ALL, ALL, yl, high_cols(None))
-    yb = send(3, hi, hi, y_dev)
+    block[pl.ds(0, 64), :] = high
+    block[pl.ds(64, 64), :] = (folded - high.astype(f32)).astype(bf16)
+
+    u_blocks.start()
+    norm_rows(48, 16)
+    d3[3].forward()
+    e3[3].forward()
+    e_blocks.arrive()
+    e_blocks.ring()
+    u_blocks.across()
 
     table = dot3(bias_in[...], onehot[...])
     for h in range(8):
         row = jnp.broadcast_to(table[h : h + 1], (SEQ, 512))
         bias[h] = pltpu.roll(row, 0, 1, stride=1, stride_axis=0)[:, :SEQ]
-
-    for m in range(NMP):
-        got = remote(block, e(m, yl, z), send_sem.at[36], recv_sem.at[40 + m], y_dev)
-        pl.when(jnp.logical_not(jnp.logical_and(mine, m == mp)))(got.wait_recv)
-
-    @pl.when(mine)
-    def _():
-        keep.wait()
-
-    near = pl.ds(yh * 2, 2)
-    far_half = pl.ds(2 - yh * 2, 2)
-    y1 = send(44, e(near, yl, z), e(near, yl, z), y_dev)
-    y2 = send(45, e(far_half, 1 - yl, z), e(far_half, 1 - yl, z), y_dev)
-
-    d3.forward()
-    e3.forward()
 
     def product(k, rows, xi, zi):
         at = pl.multiple_of((xi * 4 + zi) * 256, 256)
@@ -496,17 +597,19 @@
         qkv[1, rows, :] = total.astype(bf16)
 
     project(first_q)
-    y1.wait_recv()
-    y2.wait_recv()
-    e_up = [send(46 + i, e(ALL, i, z), e(ALL, i, z), dev("z", 1)) for i in range(2)]
-    e_down = [send(48 + i, e(ALL, i, z), e(ALL, i, z), dev("z", 3)) for i in (1, 0)]
+    u_blocks.along()
     project(first_k)
-    ya.wait_recv()
-    yb.wait_recv()
+    u_blocks.forward()
+    for copy in yas + ybs:
+        copy.wait_recv()
     project(all_v)
-    d3.end()
+    u_blocks.arrive()
+    u_blocks.ring()
+    for ring in d3:
+        ring.end()
     project(last_q)
-    e3.end()
+    for ring in e3:
+        ring.end()
     project(last_k)
 
     lane = lax.broadcasted_iota(jnp.int32, (SEQ, 128), 1)
@@ -565,12 +668,8 @@
     attend(1)
     hand_out(1)
     hand_on(0)
-    e_up[0].wait_recv()
-    piece = e(ALL, 0, lax.rem(z + 3, 4))
-    ef_up = send(50, piece, piece, dev("z", 1))
-    e_down[0].wait_recv()
-    piece = e(ALL, 1, lax.rem(z + 1, 4))
-    ef_down = send(51, piece, piece, dev("z", 3))
+    e_blocks.ring_forward()
+    u_blocks.ring_forward()
     attend(2)
     hand_out(2)
     hand_on(1)
@@ -581,10 +680,8 @@
     hand_over(1)
     hand_on(3)
     load_here.wait()
-    e_up[1].wait_recv()
-    e_down[1].wait_recv()
-    ef_up.wait_recv()
-    ef_down.wait_recv()
+    e_blocks.ring_end()
+    u_blocks.ring_end()
     hand_over(2)
     hand_over(3)
     def out_project(p):
@@ -595,7 +692,7 @@
             total = None
             for m in range(NMP):
                 term = jnp.dot(
-                    att[m, rows, :], e_ref[m, pl.ds(0, 512), cols], preferred_element_type=f32
+                    att[m, rows, :], e_ref[m, :, cols], preferred_element_type=f32
                 ).astype(bf16).astype(f32)
                 total = term if total is None else total + term
             enc_out[rows, cols] = (tok_here[rows, cols].astype(f32) + total).astype(bf16)
@@ -610,7 +707,7 @@
         squares = jnp.broadcast_to(squares, (SEQ, 128)).T[:8]
         for m in range(NMP):
             both = lax.dot_general(
-                e_ref[m, pl.ds(512, 128), :], enc, (((1,), (1,)), ((), ())),
+                u_ref[m], enc, (((1,), (1,)), ((), ())),
                 preferred_element_type=f32,
             )
             both = both[:64] + both[64:]
@@ -811,15 +908,16 @@
     for copy in sent:
         copy.wait_send()
     for k in range(1, 4):
-        block_copy(k).wait_send()
         for copy in to_owner(k):
             copy.wait_send()
 
     @pl.when(jnp.logical_not(mine))
     def _():
-        block_copy(0).wait_send()
         for copy in to_owner(0):
             copy.wait_send()
+
+    e_blocks.finish()
+    u_blocks.finish()
 
 
 def encoder(args):
@@ -839,12 +937,13 @@
             pltpu.VMEM((tok_rows, D), bf16),
             pltpu.VMEM((2, tok_rows, 512), jnp.float32),
             pltpu.VMEM((3, tok_rows, 512), bf16),
-            pltpu.VMEM((NMP, 640, 1024), bf16),
+            pltpu.VMEM((NMP, 512, 1024), bf16),
+            pltpu.VMEM((NMP, 128, 1024), bf16),
             pltpu.VMEM((NMP, tok_rows, 512), bf16),
             pltpu.VMEM((4, SEQ, 512), bf16),
             pltpu.VMEM((8, SEQ, SEQ), jnp.float32),
             pltpu.VMEM((tok_rows, 1024), bf16),
-            pltpu.VMEM((640, 128), bf16),
+            pltpu.VMEM((128, 128), bf16),
             pltpu.VMEM((NMP, 8, 128), jnp.float32),
             pltpu.VMEM((4, 8, 640), jnp.float32),
             pltpu.VMEM((8, 8, 640), f32),
@@ -868,8 +967,8 @@
             pltpu.VMEM((4, 8, 512), f32),
             pltpu.VMEM((8, 8, 512), f32),
             pltpu.VMEM((NMP, 8, 128), f32),
-            pltpu.SemaphoreType.DMA((136,)),
-            pltpu.SemaphoreType.DMA((136,)),
+            pltpu.SemaphoreType.DMA((230,)),
+            pltpu.SemaphoreType.DMA((230,)),
             pltpu.SemaphoreType.DMA((5,)),
         ],
         compiler_params=pltpu.CompilerParams(

time: 230 us -> 198 us (0.86)
  Pallas kernels: 226 us -> 194 us
    pallas_call x1, Pallas kernels: 223 us -> 191 us  [encoder(): pl.pallas_call(encoder_kernel, out_shape=(jax.ShapeDtypeStruct((tok_rows,...]
where the time goes in v4:
time: 198 us
  Pallas kernels  194 us (98%)
  local copies, waits for them, and re-layouts  3.66 us (2%)
    pallas_call x1, Pallas kernels, encoder(): pl.pallas_call(encoder_kernel, out_shape=(jax.ShapeDtypeStruct((tok_rows,...  191 us

profile of v4, /device:TPU:1, one launch (start us, length us, event | category | flops | bytes accessed | tf_op | source)
XLA Modules:
  0.0 197.9 jit_solution(12494261917478006979)
XLA Ops:
  0.6 2.3 %shard_map.167 = (f32[8,128]{1,0:T(8,128)}, f32[4,8,256]{2,1,0:T(8,128)}, s32[4,16,256]{2,1,0:T(8,128)}, f32[4,16,256]{2,1,0:T(8,128)}) custom-call(s32[2,4]{1,0:T(2,128)} %bitcast.8, s32[4]{0:T(128)} %lengths.1, s32[4]{0:T(128)} %assignment.1, f32[4]{0:T(128)} %retrieval.1, bf16[8032,128]{1,0:T(8,128)(2,1)} %table.1), custom_call_target="tpu_custom_call" | custom-call | tf_op jit(solution)/shard_map/pallas_call | solution.py:110
  3.0 191.3 %shard_map.168 = (bf16[1024,1024]{1,0:T(8,128)(2,1)}, bf16[8,32]{1,0:T(8,128)(2,1)}) custom-call(bf16[1024,4096]{1,0:T(8,128)(2,1)} %tokens.1, f32[1,4096]{1,0:T(1,128)} %bitcast.5, bf16[3,128,512]{2,1,0:T(8,128)(2,1)} %w_ref.1, f32[8,32]{1,0:T(8,128)} %bias_in.1, bf16[32,512]{1,0:T(8,128)(2,1)} %constant.2.clone.onehot, ...), custom_call_target="tpu_custom_call" | custom-call | tf_op jit(solution)/shard_map/pallas_call | solution.py:927
  194.3 0.0 copy-start
  194.3 3.1 %copy.20 = bf16[1024,1024]{1,0:T(8,128)(2,1)} copy(bf16[1024,1024]{1,0:T(8,128)(2,1)} %get-tuple-element.16) | data formatting | bytes 4194304
  197.4 0.0 copy-done
  197.4 0.6 copy.21
Async XLA Ops:
  194.3 3.1 %copy-start = (bf16[8,32]{1,0:T(8,128)(2,1)S(1)}, bf16[8,32]{1,0:T(8,128)(2,1)}, u32[]{:S(2)}) copy-start(bf16[8,32]{1,0:T(8,128)(2,1)} %get-tuple-element.13) | copy-start | bytes 1540

commit v5 on v4

--- a/solution.py
+++ b/solution.py
@@ -187,12 +187,7 @@
     y_zin,
     st_z,
     y_one,
-    y_ysrc,
-    y_yin,
     st_one,
-    st_yin,
-    y_two,
-    st_two,
     y_in,
     st_in,
     x_buf2,
@@ -257,8 +252,8 @@
             m = lax.rem(mp + k, NMP)
             signal((psg_of(x, jnp.where((m // 2) == yh, yl, 1 - yl), z), m))
 
-    for k in range(4):
-        frm = psg_of(lax.rem(x + k, 4), yl, z)
+    for k in range(8):
+        frm = psg_of(lax.rem(x + k, 4), lax.rem(yl + k // 4, 2), z)
         if k == 0:
             pl.when(jnp.logical_not(mine))(functools.partial(signal, (frm, x)))
         else:
@@ -420,7 +415,7 @@
     e_blocks = Blocks(188, enc_output, e_ref, 3)
     u_blocks = Blocks(209, block, u_ref, 4)
 
-    pl.semaphore_wait(pltpu.get_barrier_semaphore(), jnp.where(mine, 18, 20))
+    pl.semaphore_wait(pltpu.get_barrier_semaphore(), jnp.where(mine, 22, 24))
 
     yd = send(0, w_ref.at[0], g(0, x, z, yl), y_dev)
     ye = send(1, w_ref.at[1], g(1, x, z, yl), y_dev)
@@ -457,14 +452,14 @@
     d2 = Ring(20, "x", lambda v, c=None: g(0, v, z, None, wide(c)))
     ye.wait_recv()
     e2 = Ring(24, "z", lambda v, c=None: g(1, x, v, None, wide(c)))
+    start_d3(0, x)
+    start_e3(0, z)
     a1.end()
     a2 = Ring(12, "z", lambda v, c=None: g(2, ALL, v, yl, low_cols(c)))
     start_ya(0, z)
     b1.end()
     b2 = Ring(16, "x", lambda v, c=None: g(2, v, ALL, yl, high_cols(c)))
     start_yb(0, x)
-    start_d3(0, x)
-    start_e3(0, z)
     e_blocks.across()
 
     for copy in mps:
@@ -477,9 +472,6 @@
     xs = [send(56 + k, x_buf.at[x], x_buf.at[x], dev("x", k)) for k in range(1, 4)]
 
     e_blocks.along()
-    d2.forward(start_d3)
-    e2.forward(start_e3)
-
     load_tokens.wait()
 
     def norm_rows(first, count):
@@ -496,11 +488,15 @@
 
         lax.fori_loop(first, first + count, body, 0)
 
+    norm_rows(0, 8)
+    d2.forward(start_d3)
+    e2.forward(start_e3)
+
+    norm_rows(8, 8)
     a2.forward(start_ya)
     b2.forward(start_yb)
     d2.end(start_d3)
     e2.end(start_e3)
-    norm_rows(0, 16)
     d3[0].forward()
     e3[0].forward()
     a2.end(start_ya)
@@ -540,7 +536,6 @@
     e3[3].forward()
     e_blocks.arrive()
     e_blocks.ring()
-    u_blocks.across()
 
     table = dot3(bias_in[...], onehot[...])
     for h in range(8):
@@ -597,14 +592,13 @@
         qkv[1, rows, :] = total.astype(bf16)
 
     project(first_q)
+    u_blocks.across()
+    project(first_k)
     u_blocks.along()
-    project(first_k)
-    u_blocks.forward()
     for copy in yas + ybs:
         copy.wait_recv()
     project(all_v)
-    u_blocks.arrive()
-    u_blocks.ring()
+    u_blocks.forward()
     for ring in d3:
         ring.end()
     project(last_q)
@@ -665,15 +659,17 @@
 
     attend(0)
     hand_out(0)
+    u_blocks.arrive()
+    u_blocks.ring()
     attend(1)
     hand_out(1)
     hand_on(0)
     e_blocks.ring_forward()
-    u_blocks.ring_forward()
     attend(2)
     hand_out(2)
     hand_on(1)
     hand_over(0)
+    u_blocks.ring_forward()
     attend(3)
     hand_out(3)
     hand_on(2)
@@ -826,44 +822,42 @@
         )
         st_one[m] = both
         for i in range(2):
-            y_one[i, m] = results[i]
-    y_ysrc[...] = y_one[1 - yl].astype(bf16)
-    yc = send(110, y_ysrc, y_yin, y_dev)
-    ystc = send(111, st_one, st_yin, y_dev)
-    yc.wait_recv()
-    ystc.wait_recv()
-    for m in range(NMP):
-        both, results = merge([st_one[m], st_yin[m]], [[y_one[yl, m]], [y_yin[m]]])
-        st_two[m] = both
-        y_two[m] = results[0]
-
+            y_one[i, m] = results[i].astype(bf16)
     def to_owner(k):
-        m = lax.rem(mp + k, NMP)
-        target = (psg_of(mp, yl, z), m)
+        to_yl, m = lax.rem(yl + k // 4, 2), lax.rem(mp + k % 4, NMP)
+        target = (psg_of(mp, to_yl, z), m)
+        slot = x * 2 + yl
         return (
-            remote(y_two.at[m], y_in.at[x], send_sem.at[112 + k], recv_sem.at[112 + x], target),
-            remote(st_two.at[m], st_in.at[x], send_sem.at[116 + k], recv_sem.at[116 + x], target),
+            remote(
+                y_one.at[to_yl, m], y_in.at[slot], send_sem.at[230 + k], recv_sem.at[230 + slot], target
+            ),
+            remote(
+                st_one.at[m], st_in.at[slot], send_sem.at[238 + k], recv_sem.at[238 + slot], target
+            ),
         )
 
     def from_source(k):
-        frm = lax.rem(x + k, 4)
-        target = (psg_of(frm, yl, z), x)
+        frm, frm_yl = lax.rem(x + k, 4), lax.rem(yl + k // 4, 2)
+        target = (psg_of(frm, frm_yl, z), x)
+        slot = frm * 2 + frm_yl
         return (
-            remote(y_two.at[0], y_in.at[frm], send_sem.at[112], recv_sem.at[112 + frm], target),
-            remote(st_two.at[0], st_in.at[frm], send_sem.at[116], recv_sem.at[116 + frm], target),
+            remote(
+                y_one.at[0, 0], y_in.at[slot], send_sem.at[230], recv_sem.at[230 + slot], target
+            ),
+            remote(st_one.at[0], st_in.at[slot], send_sem.at[238], recv_sem.at[238 + slot], target),
         )
 
     @pl.when(mine)
     def _():
-        y_in[x] = y_two[mp]
-        st_in[x] = st_two[mp]
+        y_in[x * 2 + yl] = y_one[yl, mp]
+        st_in[x * 2 + yl] = st_one[mp]
 
     @pl.when(jnp.logical_not(mine))
     def _():
         for copy in to_owner(0):
             copy.start()
 
-    for k in range(1, 4):
+    for k in range(1, 8):
         for copy in to_owner(k):
             copy.start()
 
@@ -872,10 +866,10 @@
         for copy in from_source(0):
             copy.wait_recv()
 
-    for k in range(1, 4):
+    for k in range(1, 8):
         for copy in from_source(k):
             copy.wait_recv()
-    both, results = merge([st_in[j] for j in range(4)], [[y_in[j]] for j in range(4)])
+    both, results = merge([st_in[j] for j in range(8)], [[y_in[j]] for j in range(8)])
     total = jnp.broadcast_to(both[1:2], (128, 128)).T[:64]
     mean_rows = results[0] / total
     mean_rows = mean_rows * final_gain[:, pl.ds(pl.multiple_of(psg * 128, 128), 128)]
@@ -907,7 +901,7 @@
 
     for copy in sent:
         copy.wait_send()
-    for k in range(1, 4):
+    for k in range(1, 8):
         for copy in to_owner(k):
             copy.wait_send()
 
@@ -955,20 +949,15 @@
             pltpu.VMEM((4, 2, 256, 128), bf16),
             pltpu.VMEM((4, 2, 256, 128), bf16),
             pltpu.VMEM((4, NMP, 8, 128), f32),
-            pltpu.VMEM((2, NMP, 64, 128), f32),
-            pltpu.VMEM((NMP, 64, 128), bf16),
-            pltpu.VMEM((NMP, 64, 128), bf16),
+            pltpu.VMEM((2, NMP, 64, 128), bf16),
             pltpu.VMEM((NMP, 8, 128), f32),
-            pltpu.VMEM((NMP, 8, 128), f32),
-            pltpu.VMEM((NMP, 64, 128), f32),
-            pltpu.VMEM((NMP, 8, 128), f32),
-            pltpu.VMEM((4, 64, 128), f32),
-            pltpu.VMEM((4, 8, 128), f32),
+            pltpu.VMEM((8, 64, 128), bf16),
+            pltpu.VMEM((8, 8, 128), f32),
             pltpu.VMEM((4, 8, 512), f32),
             pltpu.VMEM((8, 8, 512), f32),
             pltpu.VMEM((NMP, 8, 128), f32),
-            pltpu.SemaphoreType.DMA((230,)),
-            pltpu.SemaphoreType.DMA((230,)),
+            pltpu.SemaphoreType.DMA((246,)),
+            pltpu.SemaphoreType.DMA((246,)),
             pltpu.SemaphoreType.DMA((5,)),
         ],
         compiler_params=pltpu.CompilerParams(

time: 198 us -> 193 us (0.975)
  Pallas kernels: 194 us -> 189 us
    pallas_call x1, Pallas kernels: 191 us -> 187 us  [encoder(): pl.pallas_call(encoder_kernel, out_shape=(jax.ShapeDtypeStruct((tok_rows,...]
where the time goes in v5:
time: 193 us
  Pallas kernels  189 us (98%)
  local copies, waits for them, and re-layouts  3.66 us (2%)
    pallas_call x1, Pallas kernels, encoder(): pl.pallas_call(encoder_kernel, out_shape=(jax.ShapeDtypeStruct((tok_rows,...  187 us

profile of v5, /device:TPU:1, one launch (start us, length us, event | category | flops | bytes accessed | tf_op | source)
XLA Modules:
  0.0 193.1 jit_solution(9226080682871211013)
XLA Ops:
  0.6 2.3 %shard_map.167 = (f32[8,128]{1,0:T(8,128)}, f32[4,8,256]{2,1,0:T(8,128)}, s32[4,16,256]{2,1,0:T(8,128)}, f32[4,16,256]{2,1,0:T(8,128)}) custom-call(s32[2,4]{1,0:T(2,128)} %bitcast.8, s32[4]{0:T(128)} %lengths.1, s32[4]{0:T(128)} %assignment.1, f32[4]{0:T(128)} %retrieval.1, bf16[8032,128]{1,0:T(8,128)(2,1)} %table.1), custom_call_target="tpu_custom_call" | custom-call | tf_op jit(solution)/shard_map/pallas_call | solution.py:110
  2.9 186.5 %shard_map.168 = (bf16[1024,1024]{1,0:T(8,128)(2,1)}, bf16[8,32]{1,0:T(8,128)(2,1)}) custom-call(bf16[1024,4096]{1,0:T(8,128)(2,1)} %tokens.1, f32[1,4096]{1,0:T(1,128)} %bitcast.5, bf16[3,128,512]{2,1,0:T(8,128)(2,1)} %w_ref.1, f32[8,32]{1,0:T(8,128)} %bias_in.1, bf16[32,512]{1,0:T(8,128)(2,1)} %constant.2.clone.onehot, ...), custom_call_target="tpu_custom_call" | custom-call | tf_op jit(solution)/shard_map/pallas_call | solution.py:921
  189.5 0.0 copy-start
  189.5 3.1 %copy.20 = bf16[1024,1024]{1,0:T(8,128)(2,1)} copy(bf16[1024,1024]{1,0:T(8,128)(2,1)} %get-tuple-element.16) | data formatting | bytes 4194304
  192.6 0.0 copy-done
  192.6 0.6 copy.21
Async XLA Ops:
  189.5 3.1 %copy-start = (bf16[8,32]{1,0:T(8,128)(2,1)S(1)}, bf16[8,32]{1,0:T(8,128)(2,1)}, u32[]{:S(2)}) copy-start(bf16[8,32]{1,0:T(8,128)(2,1)} %get-tuple-element.13) | copy-start | bytes 1540

commit v6 on v5

--- a/solution.py
+++ b/solution.py
@@ -162,8 +162,9 @@
     cross_output,
     claims,
     extra,
+    enc_hbm,
+    dec_out,
     enc_out,
-    dec_out,
     g_ref,
     normed,
     acc,
@@ -721,12 +722,15 @@
         sc_in[mp, p] = sc_src[mp, p]
         return out
 
-    scs = []
+    scs, leave = [], []
     for p in range(4):
         cores[p].wait_recv()
         lasts[p].wait_recv()
         out_project(p)
         scs.append(cross_scores(p))
+        rows = pl.ds(p * SEQ, SEQ)
+        leave.append(pltpu.make_async_copy(enc_out.at[rows], enc_hbm.at[rows], own_sem.at[5 + p]))
+        leave[-1].start()
 
     crosses, inverses, maxima = [], [], []
     for p in range(4):
@@ -901,6 +905,8 @@
 
     for copy in sent:
         copy.wait_send()
+    for copy in leave:
+        copy.wait()
     for k in range(1, 8):
         for copy in to_owner(k):
             copy.wait_send()
@@ -925,8 +931,9 @@
             jax.ShapeDtypeStruct((CLAIMS * POS, 32), bf16),
         ),
         in_specs=[ANY, VMEM, ANY, VMEM, VMEM, VMEM, ANY] + [VMEM] * 8,
-        out_specs=(VMEM, VMEM),
+        out_specs=(ANY, VMEM),
         scratch_shapes=[
+            pltpu.VMEM((tok_rows, 1024), bf16),
             pltpu.VMEM((3, 4, 4, 256, 512), bf16),
             pltpu.VMEM((tok_rows, D), bf16),
             pltpu.VMEM((2, tok_rows, 512), jnp.float32),
@@ -958,7 +965,7 @@
             pltpu.VMEM((NMP, 8, 128), f32),
             pltpu.SemaphoreType.DMA((246,)),
             pltpu.SemaphoreType.DMA((246,)),
-            pltpu.SemaphoreType.DMA((5,)),
+            pltpu.SemaphoreType.DMA((9,)),
         ],
         compiler_params=pltpu.CompilerParams(
             collective_id=1, has_side_effects=True, vmem_limit_bytes=58 << 20

time: 193 us -> 192 us (level)
  no operation moved by 1% of the time
where the time goes in v6:
time: 192 us
  Pallas kernels  188 us (98%)
  local copies, waits for them, and re-layouts  3.66 us (2%)
    pallas_call x1, Pallas kernels, encoder(): pl.pallas_call(encoder_kernel, out_shape=(jax.ShapeDtypeStruct((tok_rows,...  186 us

profile of v6, /device:TPU:1, one launch (start us, length us, event | category | flops | bytes accessed | tf_op | source)
XLA Modules:
  0.0 192.2 jit_solution(5275499930274003842)
XLA Ops:
  0.6 2.4 %shard_map.167 = (f32[8,128]{1,0:T(8,128)}, f32[4,8,256]{2,1,0:T(8,128)}, s32[4,16,256]{2,1,0:T(8,128)}, f32[4,16,256]{2,1,0:T(8,128)}) custom-call(s32[2,4]{1,0:T(2,128)} %bitcast.8, s32[4]{0:T(128)} %lengths.1, s32[4]{0:T(128)} %assignment.1, f32[4]{0:T(128)} %retrieval.1, bf16[8032,128]{1,0:T(8,128)(2,1)} %table.1), custom_call_target="tpu_custom_call" | custom-call | tf_op jit(solution)/shard_map/pallas_call | solution.py:110
  3.0 185.5 %shard_map.168 = (bf16[1024,1024]{1,0:T(8,128)(2,1)}, bf16[8,32]{1,0:T(8,128)(2,1)}) custom-call(bf16[1024,4096]{1,0:T(8,128)(2,1)} %tokens.1, f32[1,4096]{1,0:T(1,128)} %bitcast.5, bf16[3,128,512]{2,1,0:T(8,128)(2,1)} %w_ref.1, f32[8,32]{1,0:T(8,128)} %bias_in.1, bf16[32,512]{1,0:T(8,128)(2,1)} %constant.2.clone.onehot, ...), custom_call_target="tpu_custom_call" | custom-call | tf_op jit(solution)/shard_map/pallas_call | solution.py:927
  188.5 0.0 copy-start
  188.5 3.1 %copy.20 = bf16[1024,1024]{1,0:T(8,128)(2,1)} copy(bf16[1024,1024]{1,0:T(8,128)(2,1)} %get-tuple-element.16) | data formatting | bytes 4194304
  191.6 0.0 copy-done
  191.6 0.6 copy.21
Async XLA Ops:
  188.5 3.1 %copy-start = (bf16[8,32]{1,0:T(8,128)(2,1)S(1)}, bf16[8,32]{1,0:T(8,128)(2,1)}, u32[]{:S(2)}) copy-start(bf16[8,32]{1,0:T(8,128)(2,1)} %get-tuple-element.13) | copy-start | bytes 1540

commit v7 on v6

--- a/solution.py
+++ b/solution.py
@@ -782,6 +782,8 @@
                 lhs[p, pl.ds(m * 64 + c * 16, 16), :] = jnp.where(
                     claims[p] == c, w_mp, 0.0
                 ).astype(bf16)
+    y_copies = []
+    st_copies = [send(106 + k, all_st, st_z.at[z], dev("z", k)) for k in range(1, 4)]
     for i in range(2):
         total = None
         for p in range(4):
@@ -792,11 +794,11 @@
             total = term if total is None else total + term
         for zt in range(4):
             y_src[zt, i] = total[:, zt * 128 : (zt + 1) * 128].astype(bf16)
-    y_copies, st_copies = [], []
-    for k in range(1, 4):
-        tz = lax.rem(z + k, 4)
-        y_copies.append(send(103 + k, y_src.at[tz], y_zin.at[z], dev("z", k)))
-        st_copies.append(send(106 + k, all_st, st_z.at[z], dev("z", k)))
+        for k in range(1, 4):
+            tz = lax.rem(z + k, 4)
+            y_copies.append(
+                send((103, 110)[i] + k, y_src.at[tz, i], y_zin.at[z, i], dev("z", k))
+            )
     y_zin[z] = y_src[z]
     st_z[z] = all_st[...]
 

time: 192 us -> 192 us (level)
  no operation moved by 1% of the time
where the time goes in v7:
time: 192 us
  Pallas kernels  187 us (97%)
  local copies, waits for them, and re-layouts  3.66 us (2%)
    pallas_call x1, Pallas kernels, encoder(): pl.pallas_call(encoder_kernel, out_shape=(jax.ShapeDtypeStruct((tok_rows,...  185 us

profile of v7, /device:TPU:1, one launch (start us, length us, event | category | flops | bytes accessed | tf_op | source)
XLA Modules:
  0.0 191.5 jit_solution(1647309902845140910)
XLA Ops:
  0.6 2.3 %shard_map.167 = (f32[8,128]{1,0:T(8,128)}, f32[4,8,256]{2,1,0:T(8,128)}, s32[4,16,256]{2,1,0:T(8,128)}, f32[4,16,256]{2,1,0:T(8,128)}) custom-call(s32[2,4]{1,0:T(2,128)} %bitcast.8, s32[4]{0:T(128)} %lengths.1, s32[4]{0:T(128)} %assignment.1, f32[4]{0:T(128)} %retrieval.1, bf16[8032,128]{1,0:T(8,128)(2,1)} %table.1), custom_call_target="tpu_custom_call" | custom-call | tf_op jit(solution)/shard_map/pallas_call | solution.py:110
  3.0 184.9 %shard_map.168 = (bf16[1024,1024]{1,0:T(8,128)(2,1)}, bf16[8,32]{1,0:T(8,128)(2,1)}) custom-call(bf16[1024,4096]{1,0:T(8,128)(2,1)} %tokens.1, f32[1,4096]{1,0:T(1,128)} %bitcast.5, bf16[3,128,512]{2,1,0:T(8,128)(2,1)} %w_ref.1, f32[8,32]{1,0:T(8,128)} %bias_in.1, bf16[32,512]{1,0:T(8,128)(2,1)} %constant.2.clone.onehot, ...), custom_call_target="tpu_custom_call" | custom-call | tf_op jit(solution)/shard_map/pallas_call | solution.py:929
  187.8 0.0 copy-start
  187.9 3.1 %copy.20 = bf16[1024,1024]{1,0:T(8,128)(2,1)} copy(bf16[1024,1024]{1,0:T(8,128)(2,1)} %get-tuple-element.16) | data formatting | bytes 4194304
  190.9 0.0 copy-done
  190.9 0.6 copy.21
Async XLA Ops:
  187.8 3.1 %copy-start = (bf16[8,32]{1,0:T(8,128)(2,1)S(1)}, bf16[8,32]{1,0:T(8,128)(2,1)}, u32[]{:S(2)}) copy-start(bf16[8,32]{1,0:T(8,128)(2,1)} %get-tuple-element.13) | copy-start | bytes 1540
